TPU v7x, 32 devices: a whole 2x2x4 slice. The times are simulated.
32 devices in a mesh: dp: 8 (over z, x), replica: 4 (over y, core).
Axes of the slice: x: 2, y: 2, z: 4, core: 2. Of those that a mesh axis runs over, the one named last changes fastest.
Arguments:
- tokens: float32 [24576, 768], P(('dp', 'replica')), may hold values from -6 to 6
- patch_counts: int32 [64], replicated, may hold values from 76 to 384, as said below
- code_bits: int32 [24576, 18], P(('dp', 'replica')), may hold values from 0 to 1
- out_grad: float32 [24576, 768], P(('dp', 'replica')), may hold values from -6 to 6
- ln1_gain: float32 [768], replicated, may hold values from 0.1 to 1.9
- w_qkv: bfloat16 [768, 2304], replicated, may hold values from -0.21875 to 0.21875
- w_attn_out: bfloat16 [768, 768], replicated, may hold values from -0.875 to 0.875
- ln2_gain: float32 [768], replicated, may hold values from 0.1 to 1.9
- w_mlp_in: bfloat16 [768, 3072], replicated, may hold values from -0.21875 to 0.21875
- w_mlp_out: bfloat16 [3072, 768], replicated, may hold values from -0.109375 to 0.109375
- w_down: bfloat16 [768, 18], replicated, may hold values from -0.21875 to 0.21875
- w_up: bfloat16 [18, 768], replicated, may hold values from -1.5 to 1.5
Outputs:
- decoded: float32 [24576, 768], P(('dp', 'replica'))
- entropy_loss: float32 [], replicated
- grad_tokens: float32 [24576, 768], P(('dp', 'replica'))
- grad_ln1_gain: float32 [768], P(('dp', 'replica'))
- grad_w_qkv: float32 [768, 2304], P(('dp', 'replica'))
- grad_w_attn_out: float32 [768, 768], P(('dp', 'replica'))
- grad_ln2_gain: float32 [768], P(('dp', 'replica'))
- grad_w_mlp_in: float32 [768, 3072], P(('dp', 'replica'))
- grad_w_mlp_out: float32 [3072, 768], P(('dp', 'replica'))
- grad_w_down: float32 [768, 18], P(('dp', 'replica'))
- grad_w_up: float32 [18, 768], P(None, ('dp', 'replica'))
Inputs may be any that keep to these rules, and one draw needn't show every extreme that they name: `patch_counts`: each image holds (1 + b) * 384 // 5 patches for some b of 0 to 4; the last image holds 384.
All inputs are finite; a program needn't handle non-finite values.
Results may differ from a plain program's by a relative error of at most 0.015.
Values sent between devices are 32-bit elements; how exact they have to be, the bound alone decides.
A program may use at most 192 MiB of HBM per device.

v0:
```python
import jax
import jax.numpy as jnp
from jax import lax
from jax.sharding import PartitionSpec as P

HEADS = 12
HEAD = 64
BITS = 18
SEQ = 384


eps_norm = 1e-06
neg_big = -1e30
sharpness = 8.0
commit_weight = 0.25


def exact_gelu(values):
    return jax.nn.gelu(values, approximate=False)


def layer_norm(values, gain):
    centered = values - jnp.mean(values, axis=-1, keepdims=True)
    inv_std = lax.rsqrt(jnp.mean(centered * centered, axis=-1, keepdims=True) + eps_norm)
    normed = centered * inv_std
    return (normed * gain, normed, inv_std)


def norm_back(grad_out, normed, inv_std, gain):
    grad_normed = grad_out * gain
    grad_gain = jnp.sum(grad_out * normed, axis=0)
    spread_part = jnp.mean(grad_normed * normed, axis=-1, keepdims=True)
    grad_in = inv_std * (
        grad_normed - jnp.mean(grad_normed, axis=-1, keepdims=True) - normed * spread_part
    )
    return (grad_in, grad_gain)


def inner_rows(left, right):
    return lax.dot_general(
        left, right, (((0,), (0,)), ((), ())), preferred_element_type=jnp.float32
    )


def times_transposed(left, right):
    return lax.dot_general(
        left, right, (((1,), (1,)), ((), ())), preferred_element_type=jnp.float32
    )


def attention_logits(queries, key_rows, key_valid):
    scores = jnp.einsum("bqhd,bkhd->bhqk", queries, key_rows, preferred_element_type=jnp.float32)
    return jnp.where(key_valid, scores * HEAD ** (-0.5), neg_big)


def body(
    tokens,
    patch_counts,
    code_bits,
    out_grad,
    ln1_gain,
    w_qkv,
    w_attn_out,
    ln2_gain,
    w_mlp_in,
    w_mlp_out,
    w_down,
    w_up,
):
    row_count = tokens.shape[0]
    images = row_count // SEQ
    width_all = tokens.shape[1]
    first_image = lax.axis_index(("dp", "replica")) * images
    counts = lax.dynamic_slice_in_dim(patch_counts, first_image, images)
    total_count = jnp.sum(patch_counts).astype(jnp.float32)
    valid_slots = jnp.arange(SEQ, dtype=jnp.int32)[None, :] < counts[:, None]
    key_valid = valid_slots[:, None, None, :]
    row_valid = valid_slots.reshape(row_count).astype(jnp.float32)[:, None]
    target = (2.0 * code_bits.astype(jnp.float32) - 1.0) * BITS ** (-0.5)
    normed1_out, normed1, inv_std1 = layer_norm(tokens, ln1_gain)
    attn_in = normed1_out.astype(jnp.bfloat16)
    qkv_rows = jnp.dot(attn_in, w_qkv, preferred_element_type=jnp.float32).astype(jnp.bfloat16)
    qkv_rows = qkv_rows.reshape(images, SEQ, 3, HEADS, HEAD)
    queries = qkv_rows[:, :, 0]
    key_rows = qkv_rows[:, :, 1]
    value_rows = qkv_rows[:, :, 2]
    logits = attention_logits(queries, key_rows, key_valid)
    row_max = jnp.max(logits, axis=-1, keepdims=True)
    weights = jnp.exp(logits - row_max)
    row_total = jnp.sum(weights, axis=-1, keepdims=True)
    log_total = row_max + jnp.log(row_total)
    prob_low = (weights / row_total).astype(jnp.bfloat16)
    context = jnp.einsum(
        "bhqk,bkhd->bqhd", prob_low, value_rows, preferred_element_type=jnp.float32
    )
    context_low = context.astype(jnp.bfloat16).reshape(row_count, width_all)
    hidden1 = tokens + jnp.dot(context_low, w_attn_out, preferred_element_type=jnp.float32)
    normed2_out, normed2, inv_std2 = layer_norm(hidden1, ln2_gain)
    mlp_in = normed2_out.astype(jnp.bfloat16)
    pre_act = jnp.dot(mlp_in, w_mlp_in, preferred_element_type=jnp.float32)
    activation, gelu_back = jax.vjp(exact_gelu, pre_act)
    activation_low = activation.astype(jnp.bfloat16)
    hidden2 = hidden1 + jnp.dot(activation_low, w_mlp_out, preferred_element_type=jnp.float32)
    hidden2_low = hidden2.astype(jnp.bfloat16)
    raw_code = jnp.dot(hidden2_low, w_down, preferred_element_type=jnp.float32)
    inv_len = lax.rsqrt(jnp.sum(raw_code * raw_code, axis=-1, keepdims=True) + 1.0)
    unit_code = raw_code * inv_len
    quant_low = target.astype(jnp.bfloat16)
    decoded = row_valid * jnp.dot(quant_low, w_up, preferred_element_type=jnp.float32)
    logit_bits = unit_code * sharpness
    soft_prob = jax.nn.sigmoid(logit_bits)
    token_ent = jax.nn.softplus(logit_bits) - soft_prob * logit_bits
    code_miss = unit_code - target
    prob_sum = jnp.sum(soft_prob * row_valid, axis=0)
    ent_sum = jnp.sum(token_ent * row_valid)
    commit_sum = jnp.sum(code_miss * code_miss * row_valid)
    prob_sum, ent_sum, commit_sum = lax.psum((prob_sum, ent_sum, commit_sum), ("dp", "replica"))
    mean_prob = prob_sum / total_count
    code_ent = jnp.sum(
        -mean_prob * jnp.log(mean_prob) - (1.0 - mean_prob) * jnp.log(1.0 - mean_prob)
    )
    entropy_loss = (commit_weight * commit_sum + ent_sum) / total_count - code_ent
    grad_dec_low = (row_valid * out_grad).astype(jnp.bfloat16)
    grad_w_up = inner_rows(quant_low, grad_dec_low)
    grad_quant = times_transposed(grad_dec_low, w_up)
    prob_logit = jnp.log(mean_prob / (1.0 - mean_prob))
    loss_part = (
        sharpness * soft_prob * (1.0 - soft_prob) * (prob_logit - logit_bits)
        + 2.0 * commit_weight * code_miss
    )
    grad_unit = grad_quant + row_valid * loss_part
    grad_raw = inv_len * (
        grad_unit - unit_code * jnp.sum(grad_unit * unit_code, axis=-1, keepdims=True)
    )
    grad_raw_low = grad_raw.astype(jnp.bfloat16)
    grad_w_down = inner_rows(hidden2_low, grad_raw_low)
    grad_hidden2 = times_transposed(grad_raw_low, w_down)
    grad_mlp_low = grad_hidden2.astype(jnp.bfloat16)
    grad_w_mlp_out = inner_rows(activation_low, grad_mlp_low)
    grad_activation = times_transposed(grad_mlp_low, w_mlp_out)
    grad_pre_low = gelu_back(grad_activation)[0].astype(jnp.bfloat16)
    grad_w_mlp_in = inner_rows(mlp_in, grad_pre_low)
    grad_norm2_in = times_transposed(grad_pre_low, w_mlp_in)
    grad_from_norm2, grad_ln2 = norm_back(grad_norm2_in, normed2, inv_std2, ln2_gain)
    grad_hidden1 = grad_hidden2 + grad_from_norm2
    grad_attn_low = grad_hidden1.astype(jnp.bfloat16)
    grad_w_attn_out = inner_rows(context_low, grad_attn_low)
    grad_context = times_transposed(grad_attn_low, w_attn_out).astype(jnp.bfloat16)
    grad_context = grad_context.reshape(images, SEQ, HEADS, HEAD)
    grad_values = jnp.einsum(
        "bhqk,bqhd->bkhd", prob_low, grad_context, preferred_element_type=jnp.float32
    )
    grad_prob = jnp.einsum(
        "bqhd,bkhd->bhqk", grad_context, value_rows, preferred_element_type=jnp.float32
    )
    attn_prob = jnp.exp(attention_logits(queries, key_rows, key_valid) - log_total)
    grad_scores = (
        attn_prob
        * (grad_prob - jnp.sum(grad_prob * attn_prob, axis=-1, keepdims=True))
        * HEAD ** (-0.5)
    )
    grad_scores_low = grad_scores.astype(jnp.bfloat16)
    grad_queries = jnp.einsum(
        "bhqk,bkhd->bqhd", grad_scores_low, key_rows, preferred_element_type=jnp.float32
    )
    grad_keys = jnp.einsum(
        "bhqk,bqhd->bkhd", grad_scores_low, queries, preferred_element_type=jnp.float32
    )
    grad_qkv = jnp.stack((grad_queries, grad_keys, grad_values), axis=2).reshape(
        row_count, 3 * width_all
    )
    grad_qkv_low = grad_qkv.astype(jnp.bfloat16)
    grad_w_qkv = inner_rows(attn_in, grad_qkv_low)
    grad_norm1_in = times_transposed(grad_qkv_low, w_qkv)
    grad_from_norm1, grad_ln1 = norm_back(grad_norm1_in, normed1, inv_std1, ln1_gain)
    grad_tokens = grad_hidden1 + grad_from_norm1
    summed = (
        lax.psum_scatter(grad_ln1, ("dp", "replica"), scatter_dimension=0, tiled=True),
        lax.psum_scatter(grad_w_qkv, ("dp", "replica"), scatter_dimension=0, tiled=True),
        lax.psum_scatter(grad_w_attn_out, ("dp", "replica"), scatter_dimension=0, tiled=True),
        lax.psum_scatter(grad_ln2, ("dp", "replica"), scatter_dimension=0, tiled=True),
        lax.psum_scatter(grad_w_mlp_in, ("dp", "replica"), scatter_dimension=0, tiled=True),
        lax.psum_scatter(grad_w_mlp_out, ("dp", "replica"), scatter_dimension=0, tiled=True),
        lax.psum_scatter(grad_w_down, ("dp", "replica"), scatter_dimension=0, tiled=True),
        lax.psum_scatter(grad_w_up, ("dp", "replica"), scatter_dimension=1, tiled=True),
    )
    grad_scale = (row_count * lax.axis_size(("dp", "replica"))) ** (-0.5)
    return (
        decoded,
        entropy_loss,
        grad_tokens,
        summed[0] * grad_scale,
        summed[1] * grad_scale,
        summed[2] * grad_scale,
        summed[3] * grad_scale,
        summed[4] * grad_scale,
        summed[5] * grad_scale,
        summed[6] * grad_scale,
        summed[7] * grad_scale,
    )


def solution(mesh):
    in_specs = (
        P(("dp", "replica"), None),
        P(),
        P(("dp", "replica"), None),
        P(("dp", "replica"), None),
        P(),
        P(),
        P(),
        P(),
        P(),
        P(),
        P(),
        P(),
    )
    out_specs = (
        P(("dp", "replica"), None),
        P(),
        P(("dp", "replica"), None),
        P(("dp", "replica")),
        P(("dp", "replica"), None),
        P(("dp", "replica"), None),
        P(("dp", "replica")),
        P(("dp", "replica"), None),
        P(("dp", "replica"), None),
        P(("dp", "replica"), None),
        P(None, ("dp", "replica")),
    )
    return jax.shard_map(body, mesh=mesh, in_specs=in_specs, out_specs=out_specs, check_vma=False)
```

profile of v0, /device:TPU:0, one launch (start us, length us, event | category | flops | bytes accessed | tf_op | source)
XLA Modules:
  0.0 774.9 jit_solution(15499770111758813318)
XLA Ops:
  7.2 1.4 reduce_sum.179
  10.6 3.0 copy.62
  13.6 1.8 reduce_sum.171
  16.2 2.0 multiply_reduce_fusion.6
  18.8 6.7 convolution_convert_fusion
  25.5 5.7 copy.56
  31.3 7.9 %reshape.126 = bf16[2,384,3,12,64]{1,0,4,3,2:T(2,128)(2,1)} reshape(bf16[768,2304]{0,1:T(8,128)(2,1)} %copy.56) | data formatting | bytes 7077888 | tf_op jit(solution)/shard_map/reshape | solution.py:83
  39.2 3.9 fusion.93
  43.1 7.0 fusion.11
  50.2 8.1 %fusion.2 = f32[2,12,384]{2,1,0:T(8,128)S(1)} fusion(f32[2,12,384,384]{2,3,1,0:T(8,128)} %get-tuple-element.68, f32[2,12,384]{2,1,0:T(8,128)S(1)} %get-tuple-element.67, pred[2,384]{1,0:T(4,128)(4,1)S(1)} %get-tuple-element.65), kind=kLoop, calls=%fused_computation.9 | loop fusion | flops 14146560 | bytes 14230272 | tf_op jit(solution)/shard_map/reduce_sum | solution.py:90
  58.3 7.4 divide_convert_fusion
  67.0 1.5 copy-done.1
  72.6 27.5 %multiply_convert_fusion.1 = (bf16[768,3072]{1,0:T(8,128)(2,1)}, f32[768,3072]{1,0:T(8,128)}, f32[768,3072]{1,0:T(8,128)}) fusion(bf16[768,3072]{1,0:T(8,128)(2,1)S(1)} %bitcast.83, f32[768,768]{0,1:T(8,128)S(1)} %get-tuple-element.70, f32[768]{0:T(1024)S(1)} %copy-done.30, f32[768]{0:T(1024)S(1)} %add_rsqrt_fusion.1, f32[768]{0:T(1024)S(1)} %broadcast_multiply_fusion.9), kind=kOutput, calls=%fused_computation.12 | convolution fusion | flops 3779592192 | bytes 30680064 | tf_op jit(solution)/shard_map/dot_general | solution.py:100
  100.2 6.5 add_convert_fusion.1
  109.9 42.2 %psum.23 = f32[18]{0:T(128)} all-reduce(f32[18]{0:T(128)} %get-tuple-element.50), channel_id=1, replica_groups=mesh['dp'=8,'replica'=4] {'dp','replica'}, use_global_device_ids=true, to_apply=%region_13.14 | all-reduce | flops 18 | bytes 144 | tf_op jit(solution)/shard_map/psum | solution.py:117
  154.1 1.8 multiply_reduce_fusion.9
  157.4 2.4 fusion.96
  160.0 2.7 fusion.95
  162.6 3.2 copy.64
  165.9 13.0 %add_convert_fusion = bf16[768,3072]{1,0:T(8,128)(2,1)S(1)} fusion(f32[768,3072]{1,0:T(8,128)} %get-tuple-element.61, f32[768,3072]{1,0:T(8,128)} %get-tuple-element.71, bf16[3072,768]{1,0:T(8,128)(2,1)} %param.21, f32[768,768]{1,0:T(8,128)} %fusion.95), kind=kOutput, calls=%fused_computation.11 | convolution fusion | flops 3657498624 | bytes 30670848 | tf_op jit(solution)/shard_map/dot_general | solution.py:46
  178.9 8.5 %multiply_reduce_fusion.1 = (f32[768]{0:T(1024)}, f32[768]{0:T(1024)S(1)}, f32[768]{0:T(1024)S(1)}, f32[768,768]{0,1:T(8,128)S(1)}) fusion(f32[768,768]{0,1:T(8,128)S(1)} %copy-done.7, f32[768]{0:T(1024)S(1)} %copy-done.29, f32[768]{0:T(1024)S(1)} %broadcast_multiply_fusion.9, f32[768]{0:T(1024)S(1)} %copy-done.31, ...), kind=kOutput, calls=%fused_computation.39 | convolution fusion | flops 3628594944 | bytes 14174208 | tf_op jit(solution)/shard_map/dot_general | solution.py:46
  189.6 2.5 fusion.52
  192.2 4.2 convolution_convert_fusion.3
  196.4 2.6 copy.65
  199.0 3.6 reshape.128
  202.5 1.5 log_add_fusion
  204.0 8.8 %fusion.48 = f32[2,12,384,384]{2,3,1,0:T(8,128)} fusion(bf16[2,384,1,12,64]{1,0,4,3,2:T(2,128)(2,1)} %copy-done.5, bf16[2,384,12,64]{1,0,3,2:T(2,128)(2,1)} %reshape.128), kind=kOutput, calls=%fused_computation.70 | convolution fusion | flops 452984832 | bytes 16515072 | tf_op jit(solution)/shard_map/bqhd,bkhd->bhqk/dot_general | solution.py:153
  212.8 22.1 %fusion.43 = bf16[2,384,1,12,64]{1,4,3,0,2:T(8,128)(2,1)} fusion(f32[2,12,384,384]{2,3,1,0:T(8,128)} %fusion.48, f32[2,12,384,384]{2,3,1,0:T(8,128)} %get-tuple-element.68, f32[2,12,384]{2,1,0:T(8,128)} %log_add_fusion, pred[2,384]{1,0:T(4,128)(4,1)S(1)} %get-tuple-element.65, bf16[2,384,1,12,64]{1,0,4,3,2:T(2,128)(2,1)} %copy-done.13), kind=kOutput, calls=%fused_computation.63 | convolution fusion | flops 492512640 | bytes 30708480 | tf_op jit(solution)/shard_map/bhqk,bkhd->bqhd/dot_general | solution.py:163
  234.9 25.3 %fusion.40 = bf16[2,384,1,12,64]{1,4,3,0,2:T(8,128)(2,1)} fusion(f32[2,12,384,384]{2,3,1,0:T(8,128)} %fusion.48, f32[2,12,384,384]{2,3,1,0:T(8,128)} %get-tuple-element.68, f32[2,12,384]{2,1,0:T(8,128)} %log_add_fusion, pred[2,384]{1,0:T(4,128)(4,1)S(1)} %get-tuple-element.65, bf16[2,384,1,12,64]{1,0,4,3,2:T(2,128)(2,1)} %copy-done.12), kind=kOutput, calls=%fused_computation.62 | convolution fusion | flops 492512640 | bytes 30708480 | tf_op jit(solution)/shard_map/bhqk,bqhd->bkhd/dot_general | solution.py:166
  260.1 6.1 fusion.47
  267.1 3.6 copy.71
  271.4 1.8 copy-done.14
  273.1 5.2 fusion.89
  278.5 10.7 %fusion.55 = f32[3072,768]{1,0:T(8,128)} fusion(bf16[768,3072]{1,0:T(8,128)(2,1)} %get-tuple-element.60, f32[768,768]{1,0:T(8,128)} %fusion.95), kind=kOutput, calls=%fused_computation.77 | convolution fusion | flops 3624468480 | bytes 16515072 | tf_op jit(solution)/shard_map/dot_general | solution.py:40
  289.5 10.7 %fusion.90 = f32[768,3072]{1,0:T(8,128)} fusion(bf16[768,3072]{1,0:T(8,128)(2,1)} %copy-done.35, f32[768,768]{0,1:T(8,128)} %copy-done.6, f32[768]{0:T(1024)} %param.19, f32[768]{0:T(1024)} %copy-done.28, f32[768]{0:T(1024)S(1)} %broadcast_multiply_fusion.9), kind=kOutput, calls=%fused_computation.134 | convolution fusion | flops 3626237952 | bytes 16524288 | tf_op jit(solution)/shard_map/dot_general | solution.py:40
  300.3 2.2 fusion.66
  302.5 7.3 multiply_reduce_fusion.2
  309.8 42.0 %all-reduce.4 = (f32[]{:T(128)}, f32[]{:T(128)}, f32[768]{0:T(1024)}, f32[768]{0:T(1024)}, f32[18,768]{1,0:T(8,128)}) all-reduce(f32[]{:T(128)} %get-tuple-element.52, f32[]{:T(128)} %get-tuple-element.51, f32[768]{0:T(1024)} %get-tuple-element.46, f32[768]{0:T(1024)} %get-tuple-element.44, ...), channel_id=1, replica_groups=mesh['dp'=8,'replica'=4] {'dp','replica'}, use_global_device_ids=true, to_apply=%region_8.9 | all-reduce | flops 15362 | bytes 122896 | tf_op jit(solution)/shard_map/psum | solution.py:117
  354.5 5.2 multiply_add_fusion
  359.7 3.0 copy.72
  367.4 2.8 convolution_multiply_fusion
  371.6 1.5 broadcast_multiply_fusion.3
  373.1 109.9 %reduce-scatter.9.cloned.1.call-done = f32[24,2304]{1,0:T(8,128)} async-done(((f32[768,2304]{1,0:T(8,128)}), f32[24,2304]{1,0:T(8,128)}) %reduce-scatter.9.cloned.1.call-update) | async-done | bytes 221200 | tf_op jit(solution)/shard_map/reduce_scatter | solution.py:179
  483.0 1.6 broadcast_multiply_fusion.2
  484.7 139.9 %reduce-scatter.15.cloned.1.call-done = f32[96,768]{1,0:T(8,128)} async-done(((f32[3072,768]{1,0:T(8,128)}), f32[96,768]{1,0:T(8,128)}) %reduce-scatter.15.cloned.1.call-update) | async-done | bytes 294928 | tf_op jit(solution)/shard_map/reduce_scatter | solution.py:183
  624.6 1.7 broadcast_multiply_fusion
  626.3 138.7 %reduce-scatter.13.cloned.1.call-done = f32[24,3072]{1,0:T(8,128)} async-done(((f32[768,3072]{1,0:T(8,128)}), f32[24,3072]{1,0:T(8,128)}) %reduce-scatter.13.cloned.1.call-update) | async-done | bytes 294928 | tf_op jit(solution)/shard_map/reduce_scatter | solution.py:182
  765.0 1.7 broadcast_multiply_fusion.1
  (121 shorter events, 25.5 us)
Async XLA Ops:
  7.2 11.6 %copy-start = (bf16[768,2304]{1,0:T(8,128)(2,1)S(1)}, bf16[768,2304]{1,0:T(8,128)(2,1)}, u32[]{:S(2)}) copy-start(bf16[768,2304]{1,0:T(8,128)(2,1)} %param.17) | copy-start | bytes 10616836
  7.2 363.1 %reduce-scatter.17.cloned.1.call-start = ((), (), s32[]{:S(2)}) async-start(), calls=%async_computation.9 | async-start | bytes 405504
  15.5 10.0 %copy-start.24 = (f32[768]{0:T(1024)}, f32[768]{0:T(1024)S(1)}, u32[]{:S(2)}) copy-start(f32[768]{0:T(1024)S(1)} %broadcast_multiply_fusion.10) | copy-start | bytes 9220
  18.2 0.6 copy-start.26
  43.1 7.1 copy-start.12
  43.1 7.0 copy-start.13
  43.1 22.6 %copy-start.5 = (bf16[2,384,1,12,64]{1,0,4,3,2:T(2,128)(2,1)}, bf16[2,384,1,12,64]{1,0,4,3,2:T(2,128)(2,1)S(1)}, u32[]{:S(2)}) copy-start(bf16[2,384,1,12,64]{1,0,4,3,2:T(2,128)(2,1)S(1)} %get-tuple-element.62) | copy-start | bytes 3538948
  50.2 8.1 %copy-start.18 = (f32[2,12,384]{2,1,0:T(8,128)}, f32[2,12,384]{2,1,0:T(8,128)S(1)}, u32[]{:S(2)}) copy-start(f32[2,12,384]{2,1,0:T(8,128)S(1)} %get-tuple-element.67) | copy-start | bytes 110596
  58.3 7.5 copy-start.21
  65.7 2.8 copy-start.1
  68.6 1.7 copy-start.2
  68.6 2.0 copy-start.34
  69.8 2.8 slice-start.2
  70.0 1.8 copy-start.10
  70.6 2.1 copy-start.30
  70.6 2.1 slice-start.3
  70.6 29.6 %slice-start = ((s8[4718592]{0:T(1024)(128)(4,1)}), s8[4194304]{0:T(1024)(128)(4,1)S(1)}, s32[]{:S(2)}) async-start(s8[4718592]{0:T(1024)(128)(4,1)} %bitcast.80), calls=%async_computation.10 | async-start | bytes 8388608
  71.8 28.3 %copy-start.6 = (f32[768,768]{0,1:T(8,128)}, f32[768,768]{0,1:T(8,128)S(1)}, u32[]{:S(2)}) copy-start(f32[768,768]{0,1:T(8,128)S(1)} %get-tuple-element.70) | copy-start | bytes 7077892
  72.6 27.5 %copy-start.28 = (f32[768]{0:T(1024)}, f32[768]{0:T(1024)S(1)}, u32[]{:S(2)}) copy-start(f32[768]{0:T(1024)S(1)} %add_rsqrt_fusion.1) | copy-start | bytes 9220
  72.6 27.5 %slice-start.1 = ((s8[4718592]{0:T(1024)(128)(4,1)}), s8[524288]{0:T(1024)(128)(4,1)S(1)}, s32[]{:S(2)}) async-start(s8[4718592]{0:T(1024)(128)(4,1)} %bitcast.80), calls=%async_computation.11 | async-start | bytes 1048576
  100.2 7.5 copy-start.23
  100.2 7.8 %copy-start.15 = (f32[768,768]{1,0:T(8,128)S(1)}, f32[768,768]{1,0:T(8,128)}, u32[]{:S(2)}) copy-start(f32[768,768]{1,0:T(8,128)} %param.15) | copy-start | bytes 7077892
  106.7 1.0 copy-start.9
  107.7 1.5 copy-start.20
  108.0 1.2 copy-start.19
  156.8 0.6 copy-start.22
  159.9 211.7 %reduce-scatter.11.cloned.1.call-start = ((), (), s32[]{:S(2)}) async-start(), calls=%async_computation.6 | async-start | bytes 2433024 | tf_op jit(solution)/shard_map/reduce_scatter | solution.py:180
  165.9 13.0 %copy-start.7 = (f32[768,768]{0,1:T(8,128)S(1)}, f32[768,768]{0,1:T(8,128)}, u32[]{:S(2)}) copy-start(f32[768,768]{0,1:T(8,128)} %copy-done.6) | copy-start | bytes 7077892
  165.9 13.0 %copy-start.29 = (f32[768]{0:T(1024)S(1)}, f32[768]{0:T(1024)}, u32[]{:S(2)}) copy-start(f32[768]{0:T(1024)} %copy-done.28) | copy-start | bytes 9220
  165.9 13.0 %copy-start.31 = (f32[768]{0:T(1024)S(1)}, f32[768]{0:T(1024)}, u32[]{:S(2)}) copy-start(f32[768]{0:T(1024)} %param.19) | copy-start | bytes 9220
  178.9 8.5 %copy-start.35 = (bf16[768,3072]{1,0:T(8,128)(2,1)}, bf16[768,3072]{1,0:T(8,128)(2,1)S(1)}, u32[]{:S(2)}) copy-start(bf16[768,3072]{1,0:T(8,128)(2,1)S(1)} %add_convert_fusion) | copy-start | bytes 14155780
  178.9 8.5 %copy-start.8 = (f32[768,768]{0,1:T(8,128)S(1)}, f32[768,768]{0,1:T(8,128)}, u32[]{:S(2)}) copy-start(f32[768,768]{0,1:T(8,128)} %copy.64) | copy-start | bytes 7077892
  187.5 2.1 copy-start.11
  188.2 1.4 copy-start.4
  192.1 290.9 %reduce-scatter.9.cloned.1.call-start = ((), (), s32[]{:S(2)}) async-start(), calls=%async_computation.5 | async-start | bytes 7299072 | tf_op jit(solution)/shard_map/reduce_scatter | solution.py:179
  260.1 6.1 copy-start.16
  260.1 6.1 copy-start.17
  270.7 2.4 copy-start.3
  270.7 2.4 copy-start.25
  270.7 2.4 copy-start.27
  270.7 2.4 copy-start.32
  271.4 1.8 copy-start.14
  278.4 346.2 %reduce-scatter.15.cloned.1.call-start = ((), (), s32[]{:S(2)}) async-start(), calls=%async_computation.8 | async-start | bytes 9732096 | tf_op jit(solution)/shard_map/reduce_scatter | solution.py:183
  289.2 475.8 %reduce-scatter.13.cloned.1.call-start = ((), (), s32[]{:S(2)}) async-start(), calls=%async_computation.7 | async-start | bytes 9732096 | tf_op jit(solution)/shard_map/reduce_scatter | solution.py:182
  300.3 2.3 copy-start.33
Sparse Core Ops, SparseCore 0:
  160.0 94.7 reduce-scatter.16
  260.9 98.0 reduce-scatter.10
  364.7 118.2 reduce-scatter.8
  489.8 134.7 reduce-scatter.14
  630.4 134.6 reduce-scatter.12
where the time goes:
time: 785 us; the launch traced here: 775 us
  waiting for transfers between devices  389 us (50%)
  matrix products  187 us (24%)
  blocking collectives  84.1 us (11%)
  other arithmetic  48.1 us (6%)
  local copies, waits for them, and re-layouts  47.9 us (6%)
  between operations  18.6 us (2%)
    reduce_scatter x1, waiting for transfers between devices, body(): lax.psum_scatter(grad_w_mlp_out, ('dp', 'replica'), scatter_dimension=0,...  140 us
    reduce_scatter x1, waiting for transfers between devices, body(): lax.psum_scatter(grad_w_mlp_in, ('dp', 'replica'), scatter_dimension=0, t...  139 us
    reduce_scatter x1, waiting for transfers between devices, body(): lax.psum_scatter(grad_w_qkv, ('dp', 'replica'), scatter_dimension=0, tile...  110 us
    psum x2, blocking collectives, body(): lax.psum((prob_sum, ent_sum, commit_sum), ('dp', 'replica'))  84.1 us
    dot_general x6, matrix products, times_transposed(): lax.dot_general(left, right, (((1,), (1,)), ((), ())), preferred_element_...  37.5 us
    dot_general x6, matrix products, inner_rows(): lax.dot_general(left, right, (((0,), (0,)), ((), ())), preferred_element_...  33.9 us
    dot_general x1, matrix products, body(): pre_act = jnp.dot(mlp_in, w_mlp_in, preferred_element_type=jnp.float32)  27.5 us
    dot_general x1, matrix products, body(): jnp.einsum('bhqk,bqhd->bkhd', grad_scores_low, queries, preferred_element...  25.3 us
  transfers between devices with their start and end apart: 5, of which 3 were waited for; matrix products, arithmetic and copies ran while one was open for 22% of the time, Pallas kernels for 0%

commit v1 on v0

--- a/solution.py
+++ b/solution.py
@@ -1,12 +1,513 @@
+import functools
+import math
+
 import jax
 import jax.numpy as jnp
 from jax import lax
+from jax.experimental import pallas as pl
+from jax.experimental.pallas import tpu as pltpu
 from jax.sharding import PartitionSpec as P
 
-HEADS = 12
-HEAD = 64
-BITS = 18
-SEQ = 384
+HEADS, HEAD, BITS, SEQ = 12, 64, 18, 384
+D, FF = 768, 3072
+EPS = 1e-06
+bf16, f32 = jnp.bfloat16, jnp.float32
+
+def dot(a, b, ca=1, cb=0):
+    return lax.dot_general(a, b, (((ca,), (cb,)), ((), ())), preferred_element_type=f32)
+
+def norm_stats(v):
+    mean = jnp.sum(v, axis=1, keepdims=True) * (1.0 / D)
+    cen = v - mean
+    var = jnp.sum(cen * cen, axis=1, keepdims=True) * (1.0 / D)
+    inv = lax.rsqrt(var + EPS)
+    return cen * inv, inv
+
+def cols(i, n):
+    return pl.ds(pl.multiple_of(i * n, n), n)
+
+def lanes_of(rows, width=128):
+    return lax.broadcasted_iota(jnp.int32, (rows, width), 1)
+
+def widen(bits, width=128):
+    z = jnp.zeros((bits.shape[0], 32 - BITS), bits.dtype)
+    one = jnp.concatenate([bits, z], axis=1)
+    return jnp.concatenate([one] * 4, axis=1)
+
+def gelu_parts(x):
+    cdf = 0.5 + 0.5 * lax.erf(x * math.sqrt(0.5))
+    pdf = jnp.exp(x * x * -0.5) * (1.0 / math.sqrt(2.0 * math.pi))
+    return x * cdf, cdf + x * pdf
+
+MC = 512
+def forward_kernel(counts, tokens_h, wqkv_h, wao_h, win_h, wout_h, g1, g2, wdown,
+                   qkv_h, e_h, linv_h, ctx_h, hid_h, mlpin_h, act_h, slope_h, raw_o, mc_o,
+                   tokens, wqkv, wao, win, wout, attn_in, qkv, e, linv, ctx, hid, mlpin, act, slope, wd4, sem, osem):
+    loads = [pltpu.make_async_copy(s, d, sem.at[i]) for i, (s, d) in enumerate(
+        [(tokens_h, tokens), (wqkv_h, wqkv), (wao_h, wao), (wout_h, wout), (win_h, win)])]
+    for l in loads: l.start()
+    outs = []
+    def put(src, dst):
+        cp = pltpu.make_async_copy(src, dst, osem.at[len(outs)])
+        cp.start(); outs.append(cp)
+    loads[0].wait()
+    def ln1(i, _):
+        r = cols(i, 128)
+        n, _inv = norm_stats(tokens[r, :])
+        attn_in[r, :] = (n * g1[...]).astype(bf16)
+        return 0
+    lax.fori_loop(0, 6, ln1, 0)
+    loads[1].wait()
+    def proj(i, _):
+        v = dot(attn_in[...], wqkv[:, cols(i, 256)])
+        v = v * jnp.where(i < 3, 0.125, 1.0)
+        qkv[pl.ds(pl.multiple_of(i // 3 * D, D), D), cols(i % 3, 256)] = v.astype(bf16)
+        return 0
+    lax.fori_loop(0, 9, proj, 0)
+    put(qkv, qkv_h)
+    first = (lax.axis_index("dp") * lax.axis_size("replica") + lax.axis_index("replica")) * 2
+    def att(i, _):
+        img = i // 3
+        n = counts[first + img]
+        r = pl.ds(pl.multiple_of(img * SEQ, SEQ), SEQ)
+        ok = lax.broadcasted_iota(jnp.int32, (1, SEQ), 1) < n
+        low = lanes_of(SEQ) < HEAD
+        one = jnp.ones((SEQ, 128), bf16)
+        for j in range(2):
+            o = i % 3 * 2 + j
+            q2, k2, v2 = (qkv[pl.ds(pl.multiple_of(b * D + img * SEQ, 128), SEQ), cols(o, 128)] for b in range(3))
+            zero = jnp.zeros_like(q2)
+            vo = jnp.concatenate([v2, one], axis=1)
+            res = []
+            for h in range(2):
+                q = jnp.where(low, q2, zero) if h == 0 else jnp.where(low, zero, q2)
+                s = jnp.where(ok, dot(q, k2, 1, 1), -1e30)
+                m = jnp.max(s, axis=1, keepdims=True)
+                p = jnp.exp(s - m).astype(bf16)
+                e[img * HEADS + o * 2 + h] = p
+                ov = dot(p, vo)
+                inv = 1.0 / ov[:, 128:]
+                res.append((ov[:, :128] * inv, inv))
+            cs = pl.ds(pl.multiple_of(o * 128, 128), 128)
+            ctx[r, cs] = jnp.where(low, res[0][0], res[1][0]).astype(bf16)
+            linv[r, cs] = jnp.where(low, res[0][1], res[1][1])
+        return 0
+    lax.fori_loop(0, 6, att, 0)
+    put(e, e_h); put(linv, linv_h); put(ctx, ctx_h)
+    loads[2].wait()
+    def ao(i, _):
+        r = cols(i, 256)
+        h = tokens[r, :] + dot(ctx[r, :], wao[...])
+        hid[r, :] = h
+        n, _inv = norm_stats(h)
+        mlpin[r, :] = (n * g2[...]).astype(bf16)
+        return 0
+    lax.fori_loop(0, 3, ao, 0)
+    put(hid, hid_h); put(mlpin, mlpin_h)
+    loads[3].wait()
+    wd4[...] = widen(wdown[...].astype(f32)).astype(bf16)
+    def mcf(i, _):
+        r = cols(i, 768)
+        v = dot(wout[r, :], wd4[...])
+        hi = v.astype(bf16).astype(f32)
+        mc_o[r, :] = jnp.where(lanes_of(768) % 64 < 32, hi, v - hi).astype(bf16)
+        return 0
+    lax.fori_loop(0, 4, mcf, 0)
+    loads[4].wait()
+    def mlp(i, _):
+        cs = cols(i, MC)
+        a, s = gelu_parts(dot(mlpin[...], win[:, cs]))
+        act[:, cs] = a.astype(bf16)
+        slope[:, cs] = s.astype(bf16)
+        return 0
+    lax.fori_loop(0, FF // MC, mlp, 0)
+    put(act, act_h); put(slope, slope_h)
+    raw = dot(act[...], mc_o[...])
+    raw = raw + pltpu.roll(raw, 32, 1)
+    raw_o[...] = raw + dot(hid[...].astype(bf16), wd4[...])
+    for o in outs: o.wait()
+
+def forward(counts, tokens, wqkv, wao, win, wout, g1, g2, wdown):
+    T = tokens.shape[0]
+    any_, vm = pl.BlockSpec(memory_space=pl.ANY), pl.BlockSpec(memory_space=pltpu.VMEM)
+    outs = [((3 * D, D), bf16), ((24, SEQ, SEQ), bf16), ((T, D), f32), ((T, D), bf16), ((T, D), f32), ((T, D), bf16),
+            ((T, FF), bf16), ((T, FF), bf16)]
+    return pl.pallas_call(forward_kernel,
+        out_shape=[jax.ShapeDtypeStruct(*o) for o in outs] + [jax.ShapeDtypeStruct((T, 128), f32), jax.ShapeDtypeStruct((FF, 128), bf16)],
+        in_specs=[pl.BlockSpec(memory_space=pltpu.SMEM)] + [any_] * 5 + [vm] * 3,
+        out_specs=[any_] * 8 + [vm] * 2,
+        scratch_shapes=[pltpu.VMEM((T, D), f32), pltpu.VMEM((D, 3 * D), bf16), pltpu.VMEM((D, D), bf16), pltpu.VMEM((D, FF), bf16), pltpu.VMEM((FF, D), bf16),
+            pltpu.VMEM((T, D), bf16)] + [pltpu.VMEM(*o) for o in outs] + [pltpu.VMEM((D, 128), bf16), pltpu.SemaphoreType.DMA((5,)), pltpu.SemaphoreType.DMA((8,))],
+        compiler_params=pltpu.CompilerParams(vmem_limit_bytes=63 << 20),
+        name="forward")(counts, tokens, wqkv, wao, win, wout, g1.reshape(1, D), g2.reshape(1, D), wdown)
+
+MESH = pl.DeviceIdType.MESH
+W = 256
+CHUNKS = 24
+LAGS = (0, 1, 5, 8, 10)
+
+def place():
+    dp, rp = lax.axis_index("dp"), lax.axis_index("replica")
+    return dp // 2, dp % 2, rp // 2, rp % 2
+
+def device(z, x, y, c):
+    return (z * 2 + x, y * 2 + c)
+
+def enter():
+    z, x, y, c = place()
+    bar = pltpu.get_barrier_semaphore()
+    peers = [device(z, x, y, 1 - c), device(z, 1 - x, y, c), device(z, x, 1 - y, c)]
+    peers += [device((z + d) % 4, x, y, c) for d in (1, 2, 3)]
+    for p in peers:
+        pl.semaphore_signal(bar, inc=1, device_id=p, device_id_type=MESH)
+    pl.semaphore_wait(bar, len(peers))
+
+class Scatter:
+    def __init__(self, n, bufs, result):
+        self.n = n
+        self.g, self.r0, self.r1, self.r2, self.r3, self.send, self.recv = bufs
+        self.result = result
+        self.ring = self.g.shape[0]
+        self.z, self.x, self.y, self.c = place()
+    def axes(self, par):
+        z, x, y, c = self.z, self.x, self.y, self.c
+        tx, ty = device(z, 1 - x, y, c), device(z, x, 1 - y, c)
+        return (x, y, tx, ty) if par == 0 else (y, x, ty, tx)
+    def copy(self, k, n, src, dst, to):
+        return pltpu.make_async_remote_copy(src, dst, self.send.at[k, n], self.recv.at[k, n], device_id=to, device_id_type=MESH)
+    def c0(self, k, par):
+        return self.copy(k, 0, self.g.at[par % self.ring, 1 - self.c], self.r0.at[k], device(self.z, self.x, self.y, 1 - self.c))
+    def c1(self, k, par):
+        a, b, ta, tb = self.axes(par)
+        return self.copy(k, 1, self.r0.at[k, 1 - a], self.r1.at[k], ta)
+    def c2(self, k, par):
+        a, b, ta, tb = self.axes(par)
+        return self.copy(k, 2, self.r1.at[k, 1 - b], self.r2.at[k], tb)
+    def c3(self, k, d):
+        t = (self.z + d) % 4
+        return self.copy(k, 2 + d, self.r2.at[k, t], self.r3.at[k, d - 1], device(t, self.x, self.y, self.c))
+    def put(self, par, v, lane=0):
+        for o in range(32):
+            z, x, y, c = o // 8, o // 4 % 2, o // 2 % 2, o % 2
+            a, b = (x, y) if par == 0 else (y, x)
+            self.g[par % self.ring, c, a, b, z, :, lane:lane + v.shape[1]] = v[o * 24:o * 24 + 24]
+    def step0(self, k, par):
+        self.c0(k, par).start()
+    def step1(self, k, par):
+        self.c0(k, par).wait()
+        self.r0[k] += self.g[par % self.ring, self.c]
+        self.c1(k, par).start()
+    def step2(self, k, par):
+        a, b, ta, tb = self.axes(par)
+        self.c1(k, par).wait()
+        self.r1[k] += jnp.where(a == 0, self.r0[k, 0], self.r0[k, 1])
+        self.c2(k, par).start()
+    def step3(self, k, par):
+        a, b, ta, tb = self.axes(par)
+        self.c2(k, par).wait()
+        self.r2[k] += jnp.where(b == 0, self.r1[k, 0], self.r1[k, 1])
+        for d in (1, 2, 3):
+            self.c3(k, d).start()
+    def step4(self, k, par):
+        for d in (1, 2, 3):
+            self.c3(k, d).wait()
+        z = self.z
+        own = jnp.where(z < 2, jnp.where(z == 0, self.r2[k, 0], self.r2[k, 1]), jnp.where(z == 2, self.r2[k, 2], self.r2[k, 3]))
+        self.result(k, own + self.r3[k, 0] + self.r3[k, 1] + self.r3[k, 2])
+    def tick(self, t, off, start=0, end=5):
+        for s in range(4, -1, -1):
+            if not start <= s < end:
+                continue
+            k, par = t - LAGS[s], (off - LAGS[s]) % 2
+            run = functools.partial(getattr(self, f"step{s}"), par=par)
+            if isinstance(t, int):
+                if 0 <= k < self.n:
+                    run(jnp.int32(k))
+            else:
+                pl.when(k >= 0)(functools.partial(run, k))
+
+def scatter_bufs(n, ring, w):
+    return [pltpu.VMEM((ring, 2, 2, 2, 4, 24, w), f32), pltpu.VMEM((n, 2, 2, 4, 24, w), f32), pltpu.VMEM((n, 2, 4, 24, w), f32),
+            pltpu.VMEM((n, 4, 24, w), f32), pltpu.VMEM((n, 3, 24, w), f32),
+            pltpu.SemaphoreType.DMA((n, 6)), pltpu.SemaphoreType.DMA((n, 6))]
+
+def norm_back(grad, normed, inv, gain):
+    gn = grad * gain
+    spread = jnp.sum(gn * normed, axis=1, keepdims=True) * (1.0 / D)
+    mean = jnp.sum(gn, axis=1, keepdims=True) * (1.0 / D)
+    return inv * (gn - mean - normed * spread), jnp.sum(grad * normed, axis=0, keepdims=True)
+
+def backward_kernel(counts, raw, bits, wup, wdown, g1, g2, mc,
+                    tokens_h, outgrad_h, wqkv_h, wao_h, win_h, wout_h, qkv_h, e_h, linv_h, ctx_h, hid_h, mlpin_h, act_h, slope_h,
+                    gtok_h, loss_o, grads_o, small_o, tail_o,
+                    big, wao, win, wout, e, ctx, hid, mlpin, act, slope, mlpinT, ainT, dattn, draw, drawT, unit_s,
+                    wup4, wd4, smallT, gT, quantT, gain1, st, zs, sem, ssem, rsem, esem, osem, *bufs):
+    main = Scatter(CHUNKS, bufs[0:7], lambda k, v: grads_o.__setitem__(k, v))
+    small = Scatter(1, bufs[7:14], lambda k, v: small_o.__setitem__(Ellipsis, v))
+    tail = Scatter(1, bufs[14:21], lambda k, v: tail_o.__setitem__(Ellipsis, v))
+    z, x, y, c = place()
+    names = dict(outgrad=(outgrad_h, big), mlpin=(mlpin_h, mlpin), slope=(slope_h, slope), win=(win_h, win), act=(act_h, act),
+                 hid=(hid_h, hid), wout=(wout_h, wout), ctx=(ctx_h, ctx), wao=(wao_h, wao), qkv=(qkv_h, wout.at[:3 * D]),
+                 linv=(linv_h, big), wqkv=(wqkv_h, win.at[:, :3 * D]), tokens=(tokens_h, big))
+    order = list(names)
+    loads = {n: pltpu.make_async_copy(*names[n], sem.at[i]) for i, n in enumerate(order)}
+    for n in order[:9]:
+        loads[n].start()
+    def load_e(g, img):
+        return pltpu.make_async_copy(e_h.at[pl.ds(img * HEADS + g * 4, 4)], e.at[img], esem.at[img])
+    for img in range(2):
+        load_e(0, img).start()
+    enter()
+    first = (lax.axis_index("dp") * lax.axis_size("replica") + lax.axis_index("replica")) * 2
+    n0, n1 = counts[first], counts[first + 1]
+    total = lax.fori_loop(0, counts.shape[0], lambda i, a: a + counts[i], jnp.int32(0)).astype(f32)
+    wup4[...] = jnp.zeros_like(wup4)
+    for j in range(4):
+        wup4[32 * j:32 * j + BITS, :] = wup[...].astype(f32)
+    wd4[...] = widen(wdown[...].astype(f32)).astype(bf16)
+    RB = 128
+    def live(i):
+        row = lax.broadcasted_iota(jnp.int32, (RB, 128), 0) + i * RB
+        return row < jnp.where(row < SEQ, n0, n1 + SEQ)
+    def codes(i):
+        r = cols(i, RB)
+        rawv = raw[r, :]
+        inv_len = lax.rsqrt(jnp.sum(rawv * rawv, axis=1, keepdims=True) * 0.25 + 1.0)
+        unit = rawv * inv_len
+        target = widen(2.0 * bits[r, :].astype(f32) - 1.0) * BITS ** -0.5
+        both = jnp.where(live(i) & (lanes_of(RB) % 32 < BITS), 1.0, 0.0)
+        return r, inv_len, unit, target, both
+    def count(i, sums):
+        r, inv_len, unit, target, both = codes(i)
+        zl = unit * 8.0
+        p = jax.nn.sigmoid(zl)
+        miss = unit - target
+        ent = jnp.maximum(zl, 0.0) + jnp.log1p(jnp.exp(-jnp.abs(zl))) - p * zl
+        return tuple(s + jnp.sum(v * both, axis=0, keepdims=True) for s, v in zip(sums, (p, ent, miss * miss)))
+    sums = lax.fori_loop(0, 768 // RB, count, (jnp.zeros((1, 128), f32),) * 3)
+    rows8 = lax.broadcasted_iota(jnp.int32, (8, 128), 0)
+    st[0] = jnp.where(rows8 == 0, sums[0], jnp.where(rows8 == 1, sums[1], jnp.where(rows8 == 2, sums[2], 0.0)))
+    def scopy(i, to):
+        return pltpu.make_async_remote_copy(st.at[2 * i], st.at[2 * i + 1], ssem.at[i], rsem.at[i], device_id=to, device_id_type=MESH)
+    ring = [device(z, x, y, 1 - c), device(z, 1 - x, y, c), device(z, x, 1 - y, c)]
+    def zcopy(d):
+        return pltpu.make_async_remote_copy(zs.at[z], zs.at[z], ssem.at[2 + d], rsem.at[2 + d], device_id=device((z + d) % 4, x, y, c), device_id_type=MESH)
+    def pass_on(i):
+        scopy(i, ring[i]).wait()
+        s = st[2 * i] + st[2 * i + 1]
+        if i < 2:
+            st[2 * i + 2] = s
+            scopy(i + 1, ring[i + 1]).start()
+        else:
+            zs[z] = s
+            for d in (1, 2, 3): zcopy(d).start()
+    scopy(0, ring[0]).start()
+    loads["outgrad"].wait()
+    def decode(i, _):
+        r = cols(i, RB)
+        ok = live(i)
+        for j in range(6):
+            cs = slice(j * 128, (j + 1) * 128)
+            dattn[r, cs] = jnp.where(ok, big[r, cs], 0.0).astype(bf16)
+        target = widen(2.0 * bits[r, :].astype(f32) - 1.0) * BITS ** -0.5
+        draw[r, :] = target.astype(bf16)
+        return 0
+    lax.fori_loop(0, 768 // RB, decode, 0)
+    pass_on(0)
+    wup4b = wup4[...].astype(bf16)
+    unit_s[...] = dot(dattn[...], wup4b, 1, 1)
+    pass_on(1)
+    drawT[...] = draw[...].T
+    quantT[...] = dot(drawT[...], dattn[...])
+    pass_on(2)
+    loads["mlpin"].wait()
+    mlpinT[...] = mlpin[...].T
+    for d in (1, 2, 3): zcopy(d).wait()
+    zsum = zs[0] + zs[1] + zs[2] + zs[3]
+    bit8 = lanes_of(8) % 32 < BITS
+    mean_prob = jnp.where(bit8, zsum / total, 0.5)[0:1]
+    odds = jnp.log(mean_prob / (1.0 - mean_prob))
+    g0 = lanes_of(8)[0:1] < BITS
+    code_ent = jnp.sum(jnp.where(g0, -mean_prob * jnp.log(mean_prob) - (1.0 - mean_prob) * jnp.log(1.0 - mean_prob), 0.0))
+    other = jnp.sum(jnp.where(g0, 0.25 * zsum[2:3] + zsum[1:2], 0.0))
+    loss_o[0, 0] = other / total - code_ent
+    def unit_back(i, _):
+        r, inv_len, unit, target, both = codes(i)
+        zl = unit * 8.0
+        p = jax.nn.sigmoid(zl)
+        gunit = unit_s[r, :] + both * (8.0 * p * (1.0 - p) * (odds - zl) + 0.5 * (unit - target))
+        graw = inv_len * (gunit - unit * (jnp.sum(gunit * unit, axis=1, keepdims=True) * 0.25))
+        draw[r, :] = graw.astype(bf16)
+        return 0
+    lax.fori_loop(0, 768 // RB, unit_back, 0)
+    loads["slope"].wait()
+    def mlp(i, _):
+        for j in range(2):
+            t = 2 * i + j
+            cs = cols(t, W)
+            d = dot(draw[...], mc[cs, :], 1, 1) * 0.5
+            dp = (slope[:, cs].astype(f32) * d).astype(bf16)
+            slope[:, cs] = dp
+            main.put(j, dot(mlpinT[...], dp))
+            main.tick(t, j)
+        return 0
+    lax.fori_loop(0, 6, mlp, 0)
+    drawT[...] = draw[...].T
+    loads["act"].wait()
+    gT[...] = dot(drawT[...], act[...])
+    for b in range(8):
+        t = gT[:, b * 384:(b + 1) * 384].T.reshape(4, 4, 24, 128)
+        l4 = lax.broadcasted_iota(jnp.int32, (4, 24, 128), 2) // 32
+        s = jnp.where(l4 == 0, t[:, 0], 0.0)
+        for j in range(1, 4):
+            s = jnp.where(l4 == j, t[:, j], s)
+        for o in range(4):
+            small.g[0, o % 2, b % 2, o // 2, b // 2, :, 0:128] = s[o]
+    loads["hid"].wait()
+    loads["wout"].wait()
+    gv = gT[...]
+    hi = gv.astype(bf16)
+    lo = (gv - hi.astype(f32)).astype(bf16)
+    gwd = dot(drawT[...], hid[...].astype(bf16)) + dot(hi, wout[...]) + dot(lo, wout[...])
+    loads["win"].wait()
+    loads["linv"].start()
+    loads["qkv"].start()
+    def ln2(i, gain2):
+        r = cols(i, 256)
+        dn = dot(slope[r, :], win[...], 1, 1)
+        nrm, inv = norm_stats(hid[r, :])
+        gin, gg = norm_back(dn, nrm, inv, g2[...])
+        v = gin + dot(draw[r, :], wd4[...], 1, 1) * 0.25
+        hid[r, :] = v
+        dattn[r, :] = v.astype(bf16)
+        return gain2 + gg
+    gain2 = lax.fori_loop(0, 3, ln2, jnp.zeros((1, D), f32))
+    r128 = lax.broadcasted_iota(jnp.int32, (128, D), 0)
+    smallT[...] = jnp.where(r128 < 32, gwd, jnp.where(r128 < 64, quantT[...], jnp.where(r128 == 64, gain2, 0.0)))
+    for i in range(6):
+        unit_s[i * 128:(i + 1) * 128, :] = smallT[:, i * 128:(i + 1) * 128].T
+    small.put(0, unit_s[...], 128)
+    zero = jnp.int32(0)
+    small.step0(zero, 0)
+    loads["wqkv"].start()
+    loads["ctx"].wait()
+    loads["wao"].wait()
+    loads["linv"].wait()
+    mlpinT[...] = ctx[...].T
+    def dctx(i, _):
+        r = cols(i, 256)
+        mlpin[r, :] = (dot(dattn[r, :], wao[...], 1, 1) * big[r, :]).astype(bf16)
+        return 0
+    lax.fori_loop(0, 3, dctx, 0)
+    small.step1(zero, 0)
+    loads["tokens"].start()
+    loads["qkv"].wait()
+    low = lanes_of(SEQ) < HEAD
+    loads["tokens"].wait()
+    for i in range(6):
+        r = pl.ds(i * 128, 128)
+        nrm, inv = norm_stats(big[r, :])
+        ainT[:, i * 128:(i + 1) * 128] = (nrm * g1[...]).astype(bf16).T
+    def group(g, _):
+        t = 12 + 4 * g
+        main.put(0, dot(mlpinT[...], dattn[:, cols(g, W)]))
+        main.tick(t, 0)
+        def image(img, _):
+            load_e(g, img).wait()
+            r = pl.ds(pl.multiple_of(img * SEQ, SEQ), SEQ)
+            for j in range(2):
+                o = g * 2 + j
+                q2, k2, v2 = (wout[pl.ds(pl.multiple_of(b * D + img * SEQ, 128), SEQ), cols(o, 128)] for b in range(3))
+                cs = pl.ds(pl.multiple_of(o * 128, 128), 128)
+                d2, c2 = mlpin[r, cs], ctx[r, cs]
+                prod = d2.astype(f32) * c2.astype(f32)
+                zero_ = jnp.zeros_like(q2)
+                dq = dk = dv = None
+                for h in range(2):
+                    mine = low if h == 0 else jnp.logical_not(low)
+                    pick = lambda a: jnp.where(mine, a, zero_)
+                    dh = pick(d2)
+                    ev = e[img, 2 * j + h]
+                    dd = jnp.sum(jnp.where(mine, prod, 0.0), axis=1, keepdims=True)
+                    ds = (ev.astype(f32) * (dot(dh, v2, 1, 1) - dd)).astype(bf16)
+                    a, b, cc = dot(ds, pick(k2)), dot(ds, pick(q2), 0, 0), dot(ev, dh, 0, 0)
+                    dq, dk, dv = (a, b, cc) if h == 0 else (dq + a, dk + b, dv + cc)
+                for b, v in enumerate((dq * 0.125, dk, dv)):
+                    act[r, pl.ds(pl.multiple_of(b * D + o * 128, 128), 128)] = v.astype(bf16)
+            @pl.when(g < 2)
+            def _():
+                load_e(g + 1, img).start()
+            return 0
+        lax.fori_loop(0, 2, image, 0)
+        for j in range(3):
+            main.put((1 + j) % 2, dot(ainT[...], act[:, pl.ds(pl.multiple_of(j * D + g * W, W), W)]))
+            main.tick(t + 1 + j, (1 + j) % 2)
+        return 0
+    lax.fori_loop(0, 3, group, 0)
+    small.step2(zero, 0)
+    loads["wqkv"].wait()
+    def ln1(i, gain):
+        r = cols(i, 256)
+        dn = dot(act[r, :3 * D], win[:, :3 * D], 1, 1)
+        nrm, inv = norm_stats(big[r, :])
+        gin, gg = norm_back(dn, nrm, inv, g1[...])
+        hid[r, :] += gin
+        gain1[...] += gg
+        return 0
+    gain1[...] = jnp.zeros_like(gain1)
+    lax.fori_loop(0, 3, ln1, 0)
+    gtok = pltpu.make_async_copy(hid, gtok_h, osem)
+    gtok.start()
+    small.step3(zero, 0)
+    quantT[...] = jnp.broadcast_to(gain1[...], (128, D))
+    for i in range(6):
+        unit_s[i * 128:(i + 1) * 128, :] = quantT[:, i * 128:(i + 1) * 128].T
+    tail.put(1, unit_s[...])
+    tail.step0(zero, 1)
+    for t in range(CHUNKS, CHUNKS + LAGS[4] + 1):
+        main.tick(t, t % 2)
+        if t == CHUNKS: tail.step1(zero, 1)
+        if t == CHUNKS + LAGS[2] - 1: tail.step2(zero, 1)
+        if t == CHUNKS + LAGS[3] - 1: tail.step3(zero, 1); small.step4(zero, 0)
+    tail.step4(zero, 1)
+    gtok.wait()
+
+def backward(counts, raw, bits, wup, wdown, g1, g2, mc, tokens, outgrad, wqkv, wao, win, wout, qkv, e, linv, ctx, hid, mlpin, act, slope):
+    T = 768
+    any_, vm, sm = pl.BlockSpec(memory_space=pl.ANY), pl.BlockSpec(memory_space=pltpu.VMEM), pl.BlockSpec(memory_space=pltpu.SMEM)
+    V = pltpu.VMEM
+    return pl.pallas_call(backward_kernel,
+        out_shape=[jax.ShapeDtypeStruct(s, f32) for s in [(T, D), (1, 1), (CHUNKS, 24, W), (24, 256), (24, 128)]],
+        in_specs=[sm] + [vm] * 7 + [any_] * 14,
+        out_specs=[any_, sm, vm, vm, vm],
+        scratch_shapes=[V((T, D), f32), V((D, D), bf16), V((D, FF), bf16), V((FF, D), bf16), V((2, 4, SEQ, SEQ), bf16),
+            V((T, D), bf16), V((T, D), f32), V((T, D), bf16), V((T, FF), bf16), V((T, FF), bf16), V((D, T), bf16), V((D, T), bf16),
+            V((T, D), bf16), V((T, 128), bf16), V((128, T), bf16), V((T, 128), f32),
+            V((128, D), f32), V((D, 128), bf16), V((128, D), f32), V((128, FF), f32), V((128, D), f32), V((1, D), f32), V((6, 8, 128), f32), V((4, 8, 128), f32),
+            pltpu.SemaphoreType.DMA((13,)), pltpu.SemaphoreType.DMA((6,)), pltpu.SemaphoreType.DMA((6,)), pltpu.SemaphoreType.DMA((2,)), pltpu.SemaphoreType.DMA(())]
+            + scatter_bufs(CHUNKS, 2, W) + scatter_bufs(1, 1, W) + scatter_bufs(1, 1, 128),
+        compiler_params=pltpu.CompilerParams(vmem_limit_bytes=64 << 20, collective_id=1, has_side_effects=True),
+        name="backward")(counts, raw, bits, wup, wdown, g1.reshape(1, D), g2.reshape(1, D), mc, tokens, outgrad, wqkv, wao, win, wout, qkv, e, linv, ctx, hid, mlpin, act, slope)
+
+def kernel_body(tokens, counts, bits, outgrad, g1, wqkv, wao, g2, win, wout, wdown, wup):
+    qkv, e, linv, ctx, hid, mlpin, act, slope, raw, mc = forward(counts, tokens, wqkv, wao, win, wout, g1, g2, wdown)
+    gtok, loss, grads, small, tail = backward(counts, raw, bits, wup, wdown, g1, g2, mc, tokens, outgrad, wqkv, wao, win, wout, qkv, e, linv, ctx, hid, mlpin, act, slope)
+    T = tokens.shape[0]
+    scale = (T * 32) ** -0.5
+    first = (lax.axis_index("dp") * lax.axis_size("replica") + lax.axis_index("replica")) * 2
+    cn = lax.dynamic_slice_in_dim(counts, first, 2)
+    valid = (jnp.arange(SEQ)[None] < cn[:, None]).reshape(T, 1)
+    target = ((2.0 * bits.astype(f32) - 1.0) * BITS ** -0.5).astype(bf16)
+    decoded = jnp.where(valid, jnp.dot(target, wup, preferred_element_type=f32), 0.0)
+    grads = grads * scale
+    small = small * scale
+    gwin = grads[:12].transpose(1, 0, 2).reshape(24, FF)
+    grp = grads[12:].reshape(3, 4, 24, 256)
+    gwao = grp[:, 0].transpose(1, 0, 2).reshape(24, D)
+    gwqkv = grp[:, 1:].transpose(2, 1, 0, 3).reshape(24, 3 * D)
+    G = small[:, :128].reshape(24, 4, 32)[:, :, :BITS].transpose(1, 0, 2).reshape(96, BITS)
+    gwout = jnp.dot(G, wdown.astype(f32).T, precision=lax.Precision.HIGHEST)
+    return (decoded, loss.reshape(()), gtok, tail[:, 0] * scale, gwqkv, gwao, small[:, 128 + 64], gwin, gwout, small[:, 128:128 + BITS], small[:, 160:160 + BITS].T)
 
 
 eps_norm = 1e-06
@@ -26,7 +527,7 @@
     return (normed * gain, normed, inv_std)
 
 
-def norm_back(grad_out, normed, inv_std, gain):
+def plain_norm_back(grad_out, normed, inv_std, gain):
     grad_normed = grad_out * gain
     grad_gain = jnp.sum(grad_out * normed, axis=0)
     spread_part = jnp.mean(grad_normed * normed, axis=-1, keepdims=True)
@@ -53,7 +554,7 @@
     return jnp.where(key_valid, scores * HEAD ** (-0.5), neg_big)
 
 
-def body(
+def plain_body(
     tokens,
     patch_counts,
     code_bits,
@@ -141,7 +642,7 @@
     grad_pre_low = gelu_back(grad_activation)[0].astype(jnp.bfloat16)
     grad_w_mlp_in = inner_rows(mlp_in, grad_pre_low)
     grad_norm2_in = times_transposed(grad_pre_low, w_mlp_in)
-    grad_from_norm2, grad_ln2 = norm_back(grad_norm2_in, normed2, inv_std2, ln2_gain)
+    grad_from_norm2, grad_ln2 = plain_norm_back(grad_norm2_in, normed2, inv_std2, ln2_gain)
     grad_hidden1 = grad_hidden2 + grad_from_norm2
     grad_attn_low = grad_hidden1.astype(jnp.bfloat16)
     grad_w_attn_out = inner_rows(context_low, grad_attn_low)
@@ -172,7 +673,7 @@
     grad_qkv_low = grad_qkv.astype(jnp.bfloat16)
     grad_w_qkv = inner_rows(attn_in, grad_qkv_low)
     grad_norm1_in = times_transposed(grad_qkv_low, w_qkv)
-    grad_from_norm1, grad_ln1 = norm_back(grad_norm1_in, normed1, inv_std1, ln1_gain)
+    grad_from_norm1, grad_ln1 = plain_norm_back(grad_norm1_in, normed1, inv_std1, ln1_gain)
     grad_tokens = grad_hidden1 + grad_from_norm1
     summed = (
         lax.psum_scatter(grad_ln1, ("dp", "replica"), scatter_dimension=0, tiled=True),
@@ -228,4 +729,5 @@
         P(("dp", "replica"), None),
         P(None, ("dp", "replica")),
     )
+    body = kernel_body if (mesh.shape["dp"], mesh.shape["replica"]) == (8, 4) else plain_body
     return jax.shard_map(body, mesh=mesh, in_specs=in_specs, out_specs=out_specs, check_vma=False)

time: 785 us -> 182 us (0.23); the launches traced: 775 us -> 182 us
  waiting for transfers between devices: 389 us -> 0 us
  matrix products: 187 us -> 2.97 us
  Pallas kernels: 0 us -> 162 us
  blocking collectives: 84.1 us -> 0 us
  other arithmetic: 48.1 us -> 3.35 us
  local copies, waits for them, and re-layouts: 47.9 us -> 10.6 us
  between operations: 18.6 us -> 2.46 us
    reduce_scatter x4 -> x0, waiting for transfers between devices: 389 us -> none  [the longest x1 140 us: body(): lax.psum_scatter(grad_w_mlp_out, ('dp', 'replica'), scatter_dimension=0,...]
    dot_general x24 -> x2, matrix products: 187 us -> 2.97 us  [the longest x1 1.92 us: kernel_body(): jnp.dot(target, wup, preferred_element_type=f32)]
    pallas_call x0 -> x2, Pallas kernels: none -> 162 us  [the longest x1 129 us: backward(): pl.pallas_call(backward_kernel, out_shape=[jax.ShapeDtypeStruct(s, f32) f...]
    psum x2 -> x0, blocking collectives: 84.1 us -> none  [body(): lax.psum((prob_sum, ent_sum, commit_sum), ('dp', 'replica'))]
    reduce_sum x7 -> x0, other arithmetic: 15.7 us -> none  [the longest x1 8.1 us: body(): row_total = jnp.sum(weights, axis=-1, keepdims=True)]
    mul x8 -> x2, other arithmetic: 11.8 us -> 1.86 us  [the longest x1 1.12 us: kernel_body(): grads = grads * scale]
    convert_element_type x4 -> x0, local copies, waits for them, and re-layouts: 9.56 us -> none  [the longest x1 5.74 us: body(): jnp.dot(attn_in, w_qkv, preferred_element_type=jnp.float32)]
    convert_element_type x3 -> x0, other arithmetic: 9.54 us -> none  [the longest x1 7.43 us: body(): prob_low = (weights / row_total).astype(jnp.bfloat16)]
  transfers between devices with their start and end apart: 5 -> 0, of which waited for: 3 -> 0; matrix products, arithmetic and copies ran while one was open for 22% -> 0% of each run, Pallas kernels for 0% -> 0%
where the time goes in v1:
time: 182 us
  Pallas kernels  162 us (89%)
  local copies, waits for them, and re-layouts  10.6 us (6%)
  other arithmetic  3.35 us (2%)
  matrix products  2.97 us (2%)
  between operations  2.46 us (1%)
    pallas_call x1, Pallas kernels, backward(): pl.pallas_call(backward_kernel, out_shape=[jax.ShapeDtypeStruct(s, f32) f...  129 us
    pallas_call x1, Pallas kernels, forward(): pl.pallas_call(forward_kernel, out_shape=[jax.ShapeDtypeStruct(*o) for o...  33 us
    unnamed x21, local copies, waits for them, and re-layouts  5.62 us

profile of v1, /device:TPU:0, one launch (start us, length us, event | category | flops | bytes accessed | tf_op | source)
XLA Modules:
  0.0 181.6 jit_solution(17709901441159838335)
XLA Ops:
  0.6 1.6 copy.29.wdown
  2.2 1.3 reshape.69.g1
  3.5 1.3 reshape.70.g2
  4.8 0.0 copy-start.1
  4.8 33.0 %forward.1 = (bf16[2304,768]{1,0:T(8,128)(2,1)}, bf16[24,384,384]{2,1,0:T(8,128)(2,1)}, f32[768,768]{1,0:T(8,128)}, bf16[768,768]{1,0:T(8,128)(2,1)}, f32[768,76...) custom-call(s32[64]{0:T(128)} %counts.3, ...), custom_call_target="tpu_custom_call" | custom-call | tf_op jit(solution)/shard_map/forward/pallas_call | solution.py:135
  37.8 0.0 copy-done.1
  37.8 1.0 copy.30.bits
  38.8 129.2 %backward.1 = (f32[768,768]{1,0:T(8,128)}, f32[1,1]{1,0:T(1,128)}, f32[24,24,256]{2,1,0:T(8,128)}, f32[24,256]{1,0:T(8,128)}, f32[24,128]{1,0:T(8,128)}) custom-call(s32[64]{0:T(128)} %counts.3, f32[768,128]{1,0:T(8,128)} %get-tuple-element.26.raw, s32[768,18]{1,0:T(8,128)} %copy.30.bits, bf16[18,768]{1,0:T(8,128)(2,1)} %wup.1, bf16[768,18]{1,0:T(8,128)(2,1)} %copy.29.wdown, ...), custom_call_target="tpu_custom_call" | custom-call | tf_op jit(solution)/shard_map/backward/pallas_call | solution.py:479
  168.0 0.7 broadcast_multiply_fusion.1
  168.7 1.4 slice_reduce_fusion
  170.1 0.0 copy-start.4
  170.1 1.1 broadcast_multiply_fusion
  171.2 0.0 copy-start.5
  171.3 0.0 copy-start.2
  171.3 0.0 copy-start.3
  171.4 0.1 copy.43
  171.5 0.0 copy-start
  171.5 0.8 reshape.73
  172.3 0.7 copy.40
  173.1 0.6 copy.41
  173.8 0.1 reshape.76
  173.9 0.1 copy.39
  174.0 0.1 reshape.77
  174.0 0.0 copy-done.4
  174.1 1.0 fusion.6
  175.1 0.6 slice_bitcast_fusion.1
  175.7 0.7 copy.36
  176.4 0.0 copy-done.5
  176.4 0.1 dynamic_slice.3
  176.5 0.1 iota_compare_fusion
  176.6 0.0 copy-done.2
  176.6 0.0 copy-done.3
  176.6 1.9 %convolution_select_fusion = f32[768,768]{1,0:T(8,128)} fusion(bf16[18,768]{1,0:T(8,128)(2,1)S(1)} %copy-done.3, pred[768]{0:T(1024)(128)(4,1)S(1)} %lt.27, s32[768,18]{0,1:T(8,128)S(1)} %copy-done.2), kind=kOutput, calls=%fused_computation | convolution fusion | flops 21892608 | bytes 2443008 | tf_op jit(solution)/shard_map/dot_general | solution.py:501
  179.1 0.0 copy-done
  179.1 1.4 copy.47
  (6 shorter events, 0.1 us)
Async XLA Ops:
  4.8 33.0 %copy-start.1 = (s32[768,18]{0,1:T(8,128)S(1)}, s32[768,18]{0,1:T(8,128)}, u32[]{:S(2)}) copy-start(s32[768,18]{0,1:T(8,128)} %param.14) | copy-start | bytes 165892
  170.1 3.9 %copy-start.4 = (bf16[768,18]{0,1:T(8,128)(2,1)S(1)}, bf16[768,18]{0,1:T(8,128)(2,1)}, u32[]{:S(2)}) copy-start(bf16[768,18]{0,1:T(8,128)(2,1)} %param.22) | copy-start | bytes 82948
  171.2 5.1 %copy-start.5 = (s32[64]{0:T(128)S(1)}, s32[64]{0:T(128)}, u32[]{:S(2)}) copy-start(s32[64]{0:T(128)} %counts.3) | copy-start | bytes 772
  171.3 5.3 %copy-start.2 = (s32[768,18]{0,1:T(8,128)S(1)}, s32[768,18]{0,1:T(8,128)}, u32[]{:S(2)}) copy-start(s32[768,18]{0,1:T(8,128)} %param.14) | copy-start | bytes 165892
  171.3 5.3 %copy-start.3 = (bf16[18,768]{1,0:T(8,128)(2,1)S(1)}, bf16[18,768]{1,0:T(8,128)(2,1)}, u32[]{:S(2)}) copy-start(bf16[18,768]{1,0:T(8,128)(2,1)} %wup.1) | copy-start | bytes 82948
  171.5 7.6 %copy-start = (f32[768,768]{1,0:T(8,128)S(1)}, f32[768,768]{1,0:T(8,128)}, u32[]{:S(2)}) copy-start(f32[768,768]{1,0:T(8,128)} %get-tuple-element.82) | copy-start | bytes 7077892

commit v2 on v1

--- a/solution.py
+++ b/solution.py
@@ -29,10 +29,10 @@
 def lanes_of(rows, width=128):
     return lax.broadcasted_iota(jnp.int32, (rows, width), 1)
 
-def widen(bits, width=128):
-    z = jnp.zeros((bits.shape[0], 32 - BITS), bits.dtype)
-    one = jnp.concatenate([bits, z], axis=1)
-    return jnp.concatenate([one] * 4, axis=1)
+def widen(ref, rows):
+    ref[...] = jnp.zeros_like(ref)
+    for j in range(4):
+        ref[32 * j:32 * j + BITS, :] = rows
 
 def gelu_parts(x):
     cdf = 0.5 + 0.5 * lax.erf(x * math.sqrt(0.5))
@@ -40,9 +40,9 @@
     return x * cdf, cdf + x * pdf
 
 MC = 512
-def forward_kernel(counts, tokens_h, wqkv_h, wao_h, win_h, wout_h, g1, g2, wdown,
-                   qkv_h, e_h, linv_h, ctx_h, hid_h, mlpin_h, act_h, slope_h, raw_o, mc_o,
-                   tokens, wqkv, wao, win, wout, attn_in, qkv, e, linv, ctx, hid, mlpin, act, slope, wd4, sem, osem):
+def forward_kernel(counts, tokens_h, wqkv_h, wao_h, win_h, wout_h, g1, g2, wdownT, bitsT, wup,
+                   qkv_h, e_h, linv_h, ctx_h, hid_h, mlpin_h, act_h, slope_h, dec_h, raw_o, mc_o,
+                   tokens, wqkv, wao, win, wout, attn_in, qkv, e, linv, ctx, hid, mlpin, act, slope, dec, wide, wd4, sem, osem):
     loads = [pltpu.make_async_copy(s, d, sem.at[i]) for i, (s, d) in enumerate(
         [(tokens_h, tokens), (wqkv_h, wqkv), (wao_h, wao), (wout_h, wout), (win_h, win)])]
     for l in loads: l.start()
@@ -50,11 +50,25 @@
     def put(src, dst):
         cp = pltpu.make_async_copy(src, dst, osem.at[len(outs)])
         cp.start(); outs.append(cp)
+    first = (lax.axis_index("dp") * lax.axis_size("replica") + lax.axis_index("replica")) * 2
+    n0, n1 = counts[first], counts[first + 1]
+    widen(wide, wup[...].astype(f32))
+    up = wide[...].astype(bf16)
+    widen(wide, (2.0 * bitsT[...].astype(f32) - 1.0) * BITS ** -0.5)
+    wide_t = (wide[...].T * 0.25).astype(bf16)
+    for i in range(3):
+        r = pl.ds(i * 256, 256)
+        row = lax.broadcasted_iota(jnp.int32, (256, D), 0) + i * 256
+        live = row < jnp.where(row < SEQ, n0, n1 + SEQ)
+        dec[r, :] = jnp.where(live, dot(wide_t[i * 256:(i + 1) * 256], up), 0.0)
+    put(dec, dec_h)
+    widen(wide, wdownT[...].astype(f32))
+    wd4[...] = wide[...].T.astype(bf16)
     loads[0].wait()
     def ln1(i, _):
         r = cols(i, 128)
         n, _inv = norm_stats(tokens[r, :])
-        attn_in[r, :] = (n * g1[...]).astype(bf16)
+        attn_in[r, :] = (n * g1[...].reshape(1, D)).astype(bf16)
         return 0
     lax.fori_loop(0, 6, ln1, 0)
     loads[1].wait()
@@ -65,10 +79,9 @@
         return 0
     lax.fori_loop(0, 9, proj, 0)
     put(qkv, qkv_h)
-    first = (lax.axis_index("dp") * lax.axis_size("replica") + lax.axis_index("replica")) * 2
     def att(i, _):
         img = i // 3
-        n = counts[first + img]
+        n = jnp.where(img == 0, n0, n1)
         r = pl.ds(pl.multiple_of(img * SEQ, SEQ), SEQ)
         ok = lax.broadcasted_iota(jnp.int32, (1, SEQ), 1) < n
         low = lanes_of(SEQ) < HEAD
@@ -100,12 +113,11 @@
         h = tokens[r, :] + dot(ctx[r, :], wao[...])
         hid[r, :] = h
         n, _inv = norm_stats(h)
-        mlpin[r, :] = (n * g2[...]).astype(bf16)
+        mlpin[r, :] = (n * g2[...].reshape(1, D)).astype(bf16)
         return 0
     lax.fori_loop(0, 3, ao, 0)
     put(hid, hid_h); put(mlpin, mlpin_h)
     loads[3].wait()
-    wd4[...] = widen(wdown[...].astype(f32)).astype(bf16)
     def mcf(i, _):
         r = cols(i, 768)
         v = dot(wout[r, :], wd4[...])
@@ -127,24 +139,24 @@
     raw_o[...] = raw + dot(hid[...].astype(bf16), wd4[...])
     for o in outs: o.wait()
 
-def forward(counts, tokens, wqkv, wao, win, wout, g1, g2, wdown):
+def forward(counts, tokens, wqkv, wao, win, wout, g1, g2, wdownT, bitsT, wup):
     T = tokens.shape[0]
     any_, vm = pl.BlockSpec(memory_space=pl.ANY), pl.BlockSpec(memory_space=pltpu.VMEM)
     outs = [((3 * D, D), bf16), ((24, SEQ, SEQ), bf16), ((T, D), f32), ((T, D), bf16), ((T, D), f32), ((T, D), bf16),
-            ((T, FF), bf16), ((T, FF), bf16)]
+            ((T, FF), bf16), ((T, FF), bf16), ((T, D), f32)]
     return pl.pallas_call(forward_kernel,
         out_shape=[jax.ShapeDtypeStruct(*o) for o in outs] + [jax.ShapeDtypeStruct((T, 128), f32), jax.ShapeDtypeStruct((FF, 128), bf16)],
-        in_specs=[pl.BlockSpec(memory_space=pltpu.SMEM)] + [any_] * 5 + [vm] * 3,
-        out_specs=[any_] * 8 + [vm] * 2,
+        in_specs=[pl.BlockSpec(memory_space=pltpu.SMEM)] + [any_] * 5 + [vm] * 5,
+        out_specs=[any_] * 9 + [vm] * 2,
         scratch_shapes=[pltpu.VMEM((T, D), f32), pltpu.VMEM((D, 3 * D), bf16), pltpu.VMEM((D, D), bf16), pltpu.VMEM((D, FF), bf16), pltpu.VMEM((FF, D), bf16),
-            pltpu.VMEM((T, D), bf16)] + [pltpu.VMEM(*o) for o in outs] + [pltpu.VMEM((D, 128), bf16), pltpu.SemaphoreType.DMA((5,)), pltpu.SemaphoreType.DMA((8,))],
+            pltpu.VMEM((T, D), bf16)] + [pltpu.VMEM(*o) for o in outs] + [pltpu.VMEM((128, D), f32), pltpu.VMEM((D, 128), bf16), pltpu.SemaphoreType.DMA((5,)), pltpu.SemaphoreType.DMA((9,))],
         compiler_params=pltpu.CompilerParams(vmem_limit_bytes=63 << 20),
-        name="forward")(counts, tokens, wqkv, wao, win, wout, g1.reshape(1, D), g2.reshape(1, D), wdown)
+        name="forward")(counts, tokens, wqkv, wao, win, wout, g1, g2, wdownT, bitsT, wup)
 
 MESH = pl.DeviceIdType.MESH
 W = 256
-CHUNKS = 24
-LAGS = (0, 1, 5, 8, 10)
+CHUNKS = 25
+LAGS = (0, 1, 5, 7, 9, 10)
 
 def place():
     dp, rp = lax.axis_index("dp"), lax.axis_index("replica")
@@ -153,101 +165,124 @@
 def device(z, x, y, c):
     return (z * 2 + x, y * 2 + c)
 
+def near():
+    z, x, y, c = place()
+    flip = lambda v, n: 1 - v if n else v
+    return [device(z, flip(x, n & 4), flip(y, n & 2), flip(c, n & 1)) for n in range(1, 8)]
+
+def column():
+    z, x, y, c = place()
+    return [device((z + d) % 4, x, y, c) for d in (1, 2, 3)]
+
 def enter():
-    z, x, y, c = place()
     bar = pltpu.get_barrier_semaphore()
-    peers = [device(z, x, y, 1 - c), device(z, 1 - x, y, c), device(z, x, 1 - y, c)]
-    peers += [device((z + d) % 4, x, y, c) for d in (1, 2, 3)]
+    peers = near() + column()
     for p in peers:
         pl.semaphore_signal(bar, inc=1, device_id=p, device_id_type=MESH)
     pl.semaphore_wait(bar, len(peers))
 
+def planar(k):
+    if isinstance(k, int):
+        return int(k % 4 == 0 if k <= 12 else k % 2 == 1)
+    return jnp.where(k <= 12, jnp.where(lax.rem(k, 4) == 0, 1, 0), lax.rem(k, 2))
+
 class Scatter:
-    def __init__(self, n, bufs, result):
-        self.n = n
-        self.g, self.r0, self.r1, self.r2, self.r3, self.send, self.recv = bufs
+    def __init__(self, bufs, result):
+        self.g, self.r, (self.send, self.recv) = bufs[0], bufs[1:6], bufs[6:8]
         self.result = result
-        self.ring = self.g.shape[0]
-        self.z, self.x, self.y, self.c = place()
-    def axes(self, par):
-        z, x, y, c = self.z, self.x, self.y, self.c
-        tx, ty = device(z, 1 - x, y, c), device(z, x, 1 - y, c)
-        return (x, y, tx, ty) if par == 0 else (y, x, ty, tx)
-    def copy(self, k, n, src, dst, to):
-        return pltpu.make_async_remote_copy(src, dst, self.send.at[k, n], self.recv.at[k, n], device_id=to, device_id_type=MESH)
-    def c0(self, k, par):
-        return self.copy(k, 0, self.g.at[par % self.ring, 1 - self.c], self.r0.at[k], device(self.z, self.x, self.y, 1 - self.c))
-    def c1(self, k, par):
-        a, b, ta, tb = self.axes(par)
-        return self.copy(k, 1, self.r0.at[k, 1 - a], self.r1.at[k], ta)
-    def c2(self, k, par):
-        a, b, ta, tb = self.axes(par)
-        return self.copy(k, 2, self.r1.at[k, 1 - b], self.r2.at[k], tb)
-    def c3(self, k, d):
-        t = (self.z + d) % 4
-        return self.copy(k, 2 + d, self.r2.at[k, t], self.r3.at[k, d - 1], device(t, self.x, self.y, self.c))
-    def put(self, par, v, lane=0):
+        self.at = place()
+    def route(self, k, h, n):
+        z, x, y, c = self.at
+        p, zl, zh = planar(k), z % 2, z // 2
+        tz = [(z + 1 - 2 * zl, 1 - p), (z + 2 - 4 * zh, 1 - p)]
+        first, other = (x, y) if h == 0 else (y, x)
+        def to(flip_first, flip_other, nz):
+            f, o = first + flip_first * (1 - 2 * first), other + flip_other * (1 - 2 * other)
+            return device(nz, *((f, o) if h == 0 else (o, f)), c)
+        lowz, highz = z + 1 - 2 * zl, z + 2 - 4 * zh
+        if n == 1:
+            return first, to(1, 0, z)
+        if n == 2:
+            return p * other + (1 - p) * zl, to(0, p, p * z + (1 - p) * lowz)
+        if n == 3:
+            return p * zl + (1 - p) * zh, to(0, 0, p * lowz + (1 - p) * highz)
+        return p * zh + (1 - p) * other, to(0, 1 - p, p * highz + (1 - p) * z)
+    def copy(self, k, h, n):
+        _, to = self.route(k, h, n)
+        bit = self.route(k, h, n)[0]
+        i = 2 * n - 1 + h
+        return pltpu.make_async_remote_copy(self.r[n - 1].at[k, h, 1 - bit], self.r[n].at[k, h], self.send.at[k, i], self.recv.at[k, i],
+                                            device_id=to, device_id_type=MESH)
+    def pair(self, k, slot):
+        z, x, y, c = self.at
+        return pltpu.make_async_remote_copy(self.g.at[slot, 1 - c], self.r[0].at[k], self.send.at[k, 0], self.recv.at[k, 0],
+                                            device_id=device(z, x, y, 1 - c), device_id_type=MESH)
+    def put(self, slot, p, v, h):
         for o in range(32):
             z, x, y, c = o // 8, o // 4 % 2, o // 2 % 2, o % 2
-            a, b = (x, y) if par == 0 else (y, x)
-            self.g[par % self.ring, c, a, b, z, :, lane:lane + v.shape[1]] = v[o * 24:o * 24 + 24]
-    def step0(self, k, par):
-        self.c0(k, par).start()
-    def step1(self, k, par):
-        self.c0(k, par).wait()
-        self.r0[k] += self.g[par % self.ring, self.c]
-        self.c1(k, par).start()
-    def step2(self, k, par):
-        a, b, ta, tb = self.axes(par)
-        self.c1(k, par).wait()
-        self.r1[k] += jnp.where(a == 0, self.r0[k, 0], self.r0[k, 1])
-        self.c2(k, par).start()
-    def step3(self, k, par):
-        a, b, ta, tb = self.axes(par)
-        self.c2(k, par).wait()
-        self.r2[k] += jnp.where(b == 0, self.r1[k, 0], self.r1[k, 1])
-        for d in (1, 2, 3):
-            self.c3(k, d).start()
-    def step4(self, k, par):
-        for d in (1, 2, 3):
-            self.c3(k, d).wait()
-        z = self.z
-        own = jnp.where(z < 2, jnp.where(z == 0, self.r2[k, 0], self.r2[k, 1]), jnp.where(z == 2, self.r2[k, 2], self.r2[k, 3]))
-        self.result(k, own + self.r3[k, 0] + self.r3[k, 1] + self.r3[k, 2])
-    def tick(self, t, off, start=0, end=5):
-        for s in range(4, -1, -1):
-            if not start <= s < end:
-                continue
-            k, par = t - LAGS[s], (off - LAGS[s]) % 2
-            run = functools.partial(getattr(self, f"step{s}"), par=par)
+            f, s = (x, y) if h == 0 else (y, x)
+            order = (f, s, z % 2, z // 2) if p else (f, z % 2, z // 2, s)
+            self.g[(slot, c, h, *order)] = v[o * 24:o * 24 + 24]
+    def kept(self, k, h, n):
+        bit, _ = self.route(k, h, n)
+        return jnp.where(bit == 0, self.r[n - 1][k, h, 0], self.r[n - 1][k, h, 1])
+    def step(self, s, k):
+        for h in range(2):
+            self.copy(k, h, s - 1).wait()
+            v = self.r[s - 1][k, h] + self.kept(k, h, s - 1)
+            if s == 5:
+                self.result(k, h, v)
+            else:
+                self.r[s - 1][k, h] = v
+                self.copy(k, h, s).start()
+    def begin(self, k, slot):
+        self.pair(k, slot).start()
+    def join(self, k, slot):
+        self.pair(k, slot).wait()
+        self.r[0][k] += self.g[slot, self.at[3]]
+        for h in range(2):
+            self.copy(k, h, 1).start()
+    def late(self, t):
+        for s in (5, 4, 3, 2):
+            k = t - LAGS[s]
             if isinstance(t, int):
-                if 0 <= k < self.n:
-                    run(jnp.int32(k))
+                if 0 <= k < CHUNKS:
+                    self.step(s, k)
             else:
-                pl.when(k >= 0)(functools.partial(run, k))
-
-def scatter_bufs(n, ring, w):
-    return [pltpu.VMEM((ring, 2, 2, 2, 4, 24, w), f32), pltpu.VMEM((n, 2, 2, 4, 24, w), f32), pltpu.VMEM((n, 2, 4, 24, w), f32),
-            pltpu.VMEM((n, 4, 24, w), f32), pltpu.VMEM((n, 3, 24, w), f32),
-            pltpu.SemaphoreType.DMA((n, 6)), pltpu.SemaphoreType.DMA((n, 6))]
+                pl.when(k >= 0)(functools.partial(self.step, s, k))
+    def early(self, t, slot):
+        k = t - 1
+        if isinstance(t, int):
+            if k >= 0:
+                self.join(k, 1 - slot)
+            if t < CHUNKS:
+                self.begin(t, slot)
+        else:
+            pl.when(k >= 0)(functools.partial(self.join, k, 1 - slot))
+            self.begin(t, slot)
+
+def scatter_bufs():
+    blocks = [(2,) * (5 - n) for n in range(5)]
+    return [pltpu.VMEM((2, 2, 2, 2, 2, 2, 2, 24, 128), f32)] + [pltpu.VMEM((CHUNKS,) + b + (24, 128), f32) for b in blocks] + [pltpu.SemaphoreType.DMA((CHUNKS, 9))] * 2
 
 def norm_back(grad, normed, inv, gain):
     gn = grad * gain
     spread = jnp.sum(gn * normed, axis=1, keepdims=True) * (1.0 / D)
     mean = jnp.sum(gn, axis=1, keepdims=True) * (1.0 / D)
-    return inv * (gn - mean - normed * spread), jnp.sum(grad * normed, axis=0, keepdims=True)
-
-def backward_kernel(counts, raw, bits, wup, wdown, g1, g2, mc,
+    return inv * (gn - mean - normed * spread)
+
+RB = 128
+def backward_kernel(counts, raw, bitsT, wup, wdownT, g1, g2, mc,
                     tokens_h, outgrad_h, wqkv_h, wao_h, win_h, wout_h, qkv_h, e_h, linv_h, ctx_h, hid_h, mlpin_h, act_h, slope_h,
-                    gtok_h, loss_o, grads_o, small_o, tail_o,
-                    big, wao, win, wout, e, ctx, hid, mlpin, act, slope, mlpinT, ainT, dattn, draw, drawT, unit_s,
-                    wup4, wd4, smallT, gT, quantT, gain1, st, zs, sem, ssem, rsem, esem, osem, *bufs):
-    main = Scatter(CHUNKS, bufs[0:7], lambda k, v: grads_o.__setitem__(k, v))
-    small = Scatter(1, bufs[7:14], lambda k, v: small_o.__setitem__(Ellipsis, v))
-    tail = Scatter(1, bufs[14:21], lambda k, v: tail_o.__setitem__(Ellipsis, v))
+                    gtok_h, loss_o, grads_o,
+                    big, wao, win, wout, e, ctx, hid, mlpin, act, slope, mlpinT, ainT, dattn, draw, drawT, unit_s, target,
+                    wide, wd4t, smallT, gT, quantT, s8, zs, sem, ssem, rsem, esem, osem, *bufs):
+    def result(k, h, v):
+        grads_o[k, :, h * 128:(h + 1) * 128] = v
+    main = Scatter(bufs, result)
     z, x, y, c = place()
-    names = dict(outgrad=(outgrad_h, big), mlpin=(mlpin_h, mlpin), slope=(slope_h, slope), win=(win_h, win), act=(act_h, act),
-                 hid=(hid_h, hid), wout=(wout_h, wout), ctx=(ctx_h, ctx), wao=(wao_h, wao), qkv=(qkv_h, wout.at[:3 * D]),
+    names = dict(outgrad=(outgrad_h, big), mlpin=(mlpin_h, mlpin), slope=(slope_h, slope), act=(act_h, act), hid=(hid_h, hid),
+                 wout=(wout_h, wout), win=(win_h, win), ctx=(ctx_h, ctx), wao=(wao_h, wao), qkv=(qkv_h, wout.at[:3 * D]),
                  linv=(linv_h, big), wqkv=(wqkv_h, win.at[:, :3 * D]), tokens=(tokens_h, big))
     order = list(names)
     loads = {n: pltpu.make_async_copy(*names[n], sem.at[i]) for i, n in enumerate(order)}
@@ -261,11 +296,8 @@
     first = (lax.axis_index("dp") * lax.axis_size("replica") + lax.axis_index("replica")) * 2
     n0, n1 = counts[first], counts[first + 1]
     total = lax.fori_loop(0, counts.shape[0], lambda i, a: a + counts[i], jnp.int32(0)).astype(f32)
-    wup4[...] = jnp.zeros_like(wup4)
-    for j in range(4):
-        wup4[32 * j:32 * j + BITS, :] = wup[...].astype(f32)
-    wd4[...] = widen(wdown[...].astype(f32)).astype(bf16)
-    RB = 128
+    widen(wide, (2.0 * bitsT[...].astype(f32) - 1.0) * BITS ** -0.5)
+    target[...] = wide[...].T
     def live(i):
         row = lax.broadcasted_iota(jnp.int32, (RB, 128), 0) + i * RB
         return row < jnp.where(row < SEQ, n0, n1 + SEQ)
@@ -273,35 +305,23 @@
         r = cols(i, RB)
         rawv = raw[r, :]
         inv_len = lax.rsqrt(jnp.sum(rawv * rawv, axis=1, keepdims=True) * 0.25 + 1.0)
-        unit = rawv * inv_len
-        target = widen(2.0 * bits[r, :].astype(f32) - 1.0) * BITS ** -0.5
         both = jnp.where(live(i) & (lanes_of(RB) % 32 < BITS), 1.0, 0.0)
-        return r, inv_len, unit, target, both
+        return r, inv_len, rawv * inv_len, both
     def count(i, sums):
-        r, inv_len, unit, target, both = codes(i)
+        r, inv_len, unit, both = codes(i)
         zl = unit * 8.0
         p = jax.nn.sigmoid(zl)
-        miss = unit - target
+        miss = unit - target[r, :]
         ent = jnp.maximum(zl, 0.0) + jnp.log1p(jnp.exp(-jnp.abs(zl))) - p * zl
         return tuple(s + jnp.sum(v * both, axis=0, keepdims=True) for s, v in zip(sums, (p, ent, miss * miss)))
     sums = lax.fori_loop(0, 768 // RB, count, (jnp.zeros((1, 128), f32),) * 3)
     rows8 = lax.broadcasted_iota(jnp.int32, (8, 128), 0)
-    st[0] = jnp.where(rows8 == 0, sums[0], jnp.where(rows8 == 1, sums[1], jnp.where(rows8 == 2, sums[2], 0.0)))
-    def scopy(i, to):
-        return pltpu.make_async_remote_copy(st.at[2 * i], st.at[2 * i + 1], ssem.at[i], rsem.at[i], device_id=to, device_id_type=MESH)
-    ring = [device(z, x, y, 1 - c), device(z, 1 - x, y, c), device(z, x, 1 - y, c)]
-    def zcopy(d):
-        return pltpu.make_async_remote_copy(zs.at[z], zs.at[z], ssem.at[2 + d], rsem.at[2 + d], device_id=device((z + d) % 4, x, y, c), device_id_type=MESH)
-    def pass_on(i):
-        scopy(i, ring[i]).wait()
-        s = st[2 * i] + st[2 * i + 1]
-        if i < 2:
-            st[2 * i + 2] = s
-            scopy(i + 1, ring[i + 1]).start()
-        else:
-            zs[z] = s
-            for d in (1, 2, 3): zcopy(d).start()
-    scopy(0, ring[0]).start()
+    own = x * 4 + y * 2 + c
+    s8[own] = jnp.where(rows8 == 0, sums[0], jnp.where(rows8 == 1, sums[1], jnp.where(rows8 == 2, sums[2], 0.0)))
+    def tell(ref, slot, i, to):
+        return pltpu.make_async_remote_copy(ref.at[slot], ref.at[slot], ssem.at[i], rsem.at[i], device_id=to, device_id_type=MESH)
+    tells = [tell(s8, own, i, p) for i, p in enumerate(near())]
+    for t in tells: t.start()
     loads["outgrad"].wait()
     def decode(i, _):
         r = cols(i, RB)
@@ -309,20 +329,24 @@
         for j in range(6):
             cs = slice(j * 128, (j + 1) * 128)
             dattn[r, cs] = jnp.where(ok, big[r, cs], 0.0).astype(bf16)
-        target = widen(2.0 * bits[r, :].astype(f32) - 1.0) * BITS ** -0.5
-        draw[r, :] = target.astype(bf16)
         return 0
     lax.fori_loop(0, 768 // RB, decode, 0)
-    pass_on(0)
-    wup4b = wup4[...].astype(bf16)
-    unit_s[...] = dot(dattn[...], wup4b, 1, 1)
-    pass_on(1)
-    drawT[...] = draw[...].T
-    quantT[...] = dot(drawT[...], dattn[...])
-    pass_on(2)
+    quantT[...] = dot(wide[...].astype(bf16), dattn[...])
+    for t in tells: t.wait_recv()
+    s = s8[0]
+    for i in range(1, 8):
+        s = s + s8[i]
+    zs[z] = s
+    ztells = [tell(zs, z, 7 + i, p) for i, p in enumerate(column())]
+    for t in ztells: t.start()
+    for t in tells: t.wait_send()
+    widen(wide, wup[...].astype(f32))
+    unit_s[...] = dot(dattn[...], wide[...].astype(bf16), 1, 1)
     loads["mlpin"].wait()
     mlpinT[...] = mlpin[...].T
-    for d in (1, 2, 3): zcopy(d).wait()
+    widen(wide, wdownT[...].astype(f32))
+    wd4t[...] = wide[...].astype(bf16)
+    for t in ztells: t.wait()
     zsum = zs[0] + zs[1] + zs[2] + zs[3]
     bit8 = lanes_of(8) % 32 < BITS
     mean_prob = jnp.where(bit8, zsum / total, 0.5)[0:1]
@@ -332,26 +356,31 @@
     other = jnp.sum(jnp.where(g0, 0.25 * zsum[2:3] + zsum[1:2], 0.0))
     loss_o[0, 0] = other / total - code_ent
     def unit_back(i, _):
-        r, inv_len, unit, target, both = codes(i)
+        r, inv_len, unit, both = codes(i)
         zl = unit * 8.0
         p = jax.nn.sigmoid(zl)
-        gunit = unit_s[r, :] + both * (8.0 * p * (1.0 - p) * (odds - zl) + 0.5 * (unit - target))
+        gunit = unit_s[r, :] + both * (8.0 * p * (1.0 - p) * (odds - zl) + 0.5 * (unit - target[r, :]))
         graw = inv_len * (gunit - unit * (jnp.sum(gunit * unit, axis=1, keepdims=True) * 0.25))
         draw[r, :] = graw.astype(bf16)
         return 0
     lax.fori_loop(0, 768 // RB, unit_back, 0)
     loads["slope"].wait()
+    def put(t, p, v):
+        for h in range(2):
+            main.put(t % 2, p, v[:, h * 128:(h + 1) * 128], h)
     def mlp(i, _):
-        for j in range(2):
-            t = 2 * i + j
+        for j in range(4):
+            t = 4 * i + j
             cs = cols(t, W)
             d = dot(draw[...], mc[cs, :], 1, 1) * 0.5
             dp = (slope[:, cs].astype(f32) * d).astype(bf16)
             slope[:, cs] = dp
-            main.put(j, dot(mlpinT[...], dp))
-            main.tick(t, j)
-        return 0
-    lax.fori_loop(0, 6, mlp, 0)
+            main.late(t)
+            put(j, planar(j), dot(mlpinT[...], dp))
+            main.early(t, j % 2)
+        return 0
+    lax.fori_loop(0, 3, mlp, 0)
+    main.late(12)
     drawT[...] = draw[...].T
     loads["act"].wait()
     gT[...] = dot(drawT[...], act[...])
@@ -361,35 +390,35 @@
         s = jnp.where(l4 == 0, t[:, 0], 0.0)
         for j in range(1, 4):
             s = jnp.where(l4 == j, t[:, j], s)
-        for o in range(4):
-            small.g[0, o % 2, b % 2, o // 2, b // 2, :, 0:128] = s[o]
+        unit_s[b * 96:(b + 1) * 96, :] = s.reshape(96, 128)
+    main.put(0, 1, unit_s[...], 0)
     loads["hid"].wait()
     loads["wout"].wait()
     gv = gT[...]
     hi = gv.astype(bf16)
     lo = (gv - hi.astype(f32)).astype(bf16)
     gwd = dot(drawT[...], hid[...].astype(bf16)) + dot(hi, wout[...]) + dot(lo, wout[...])
+    r128 = lax.broadcasted_iota(jnp.int32, (128, D), 0)
+    smallT[...] = jnp.where(r128 < 32, gwd, quantT[...])
+    for i in range(6):
+        unit_s[i * 128:(i + 1) * 128, :] = smallT[:, i * 128:(i + 1) * 128].T
+    main.put(0, 1, unit_s[...], 1)
+    main.early(12, 0)
     loads["win"].wait()
     loads["linv"].start()
     loads["qkv"].start()
-    def ln2(i, gain2):
+    main.late(13)
+    def ln2(i, _):
         r = cols(i, 256)
         dn = dot(slope[r, :], win[...], 1, 1)
         nrm, inv = norm_stats(hid[r, :])
-        gin, gg = norm_back(dn, nrm, inv, g2[...])
-        v = gin + dot(draw[r, :], wd4[...], 1, 1) * 0.25
+        v = norm_back(dn, nrm, inv, g2[...].reshape(1, D)) + dot(draw[r, :], wd4t[...]) * 0.25
         hid[r, :] = v
         dattn[r, :] = v.astype(bf16)
-        return gain2 + gg
-    gain2 = lax.fori_loop(0, 3, ln2, jnp.zeros((1, D), f32))
-    r128 = lax.broadcasted_iota(jnp.int32, (128, D), 0)
-    smallT[...] = jnp.where(r128 < 32, gwd, jnp.where(r128 < 64, quantT[...], jnp.where(r128 == 64, gain2, 0.0)))
-    for i in range(6):
-        unit_s[i * 128:(i + 1) * 128, :] = smallT[:, i * 128:(i + 1) * 128].T
-    small.put(0, unit_s[...], 128)
-    zero = jnp.int32(0)
-    small.step0(zero, 0)
+        return 0
+    lax.fori_loop(0, 3, ln2, 0)
     loads["wqkv"].start()
+    main.late(14)
     loads["ctx"].wait()
     loads["wao"].wait()
     loads["linv"].wait()
@@ -399,7 +428,6 @@
         mlpin[r, :] = (dot(dattn[r, :], wao[...], 1, 1) * big[r, :]).astype(bf16)
         return 0
     lax.fori_loop(0, 3, dctx, 0)
-    small.step1(zero, 0)
     loads["tokens"].start()
     loads["qkv"].wait()
     low = lanes_of(SEQ) < HEAD
@@ -407,11 +435,12 @@
     for i in range(6):
         r = pl.ds(i * 128, 128)
         nrm, inv = norm_stats(big[r, :])
-        ainT[:, i * 128:(i + 1) * 128] = (nrm * g1[...]).astype(bf16).T
+        ainT[:, i * 128:(i + 1) * 128] = (nrm * g1[...].reshape(1, D)).astype(bf16).T
     def group(g, _):
-        t = 12 + 4 * g
-        main.put(0, dot(mlpinT[...], dattn[:, cols(g, W)]))
-        main.tick(t, 0)
+        t0 = 13 + 4 * g
+        main.late(t0 + 2)
+        put(1, 1, dot(mlpinT[...], dattn[:, cols(g, W)]))
+        main.early(t0, 1)
         def image(img, _):
             load_e(g, img).wait()
             r = pl.ds(pl.multiple_of(img * SEQ, SEQ), SEQ)
@@ -437,78 +466,112 @@
             @pl.when(g < 2)
             def _():
                 load_e(g + 1, img).start()
+            main.late(t0 + 3 + img)
             return 0
         lax.fori_loop(0, 2, image, 0)
         for j in range(3):
-            main.put((1 + j) % 2, dot(ainT[...], act[:, pl.ds(pl.multiple_of(j * D + g * W, W), W)]))
-            main.tick(t + 1 + j, (1 + j) % 2)
+            put(j, j % 2, dot(ainT[...], act[:, pl.ds(pl.multiple_of(j * D + g * W, W), W)]))
+            main.early(t0 + 1 + j, j % 2)
+            if j == 1:
+                main.late(t0 + 5)
         return 0
     lax.fori_loop(0, 3, group, 0)
-    small.step2(zero, 0)
+    main.early(25, 1)
+    main.late(27)
     loads["wqkv"].wait()
-    def ln1(i, gain):
+    def ln1(i, _):
         r = cols(i, 256)
         dn = dot(act[r, :3 * D], win[:, :3 * D], 1, 1)
         nrm, inv = norm_stats(big[r, :])
-        gin, gg = norm_back(dn, nrm, inv, g1[...])
-        hid[r, :] += gin
-        gain1[...] += gg
-        return 0
-    gain1[...] = jnp.zeros_like(gain1)
+        hid[r, :] += norm_back(dn, nrm, inv, g1[...].reshape(1, D))
+        return 0
     lax.fori_loop(0, 3, ln1, 0)
     gtok = pltpu.make_async_copy(hid, gtok_h, osem)
     gtok.start()
-    small.step3(zero, 0)
-    quantT[...] = jnp.broadcast_to(gain1[...], (128, D))
-    for i in range(6):
-        unit_s[i * 128:(i + 1) * 128, :] = quantT[:, i * 128:(i + 1) * 128].T
-    tail.put(1, unit_s[...])
-    tail.step0(zero, 1)
-    for t in range(CHUNKS, CHUNKS + LAGS[4] + 1):
-        main.tick(t, t % 2)
-        if t == CHUNKS: tail.step1(zero, 1)
-        if t == CHUNKS + LAGS[2] - 1: tail.step2(zero, 1)
-        if t == CHUNKS + LAGS[3] - 1: tail.step3(zero, 1); small.step4(zero, 0)
-    tail.step4(zero, 1)
+    for t in range(28, CHUNKS + LAGS[5]):
+        main.late(t)
     gtok.wait()
 
-def backward(counts, raw, bits, wup, wdown, g1, g2, mc, tokens, outgrad, wqkv, wao, win, wout, qkv, e, linv, ctx, hid, mlpin, act, slope):
+def backward(counts, raw, bitsT, wup, wdownT, g1, g2, mc, *arrays):
     T = 768
     any_, vm, sm = pl.BlockSpec(memory_space=pl.ANY), pl.BlockSpec(memory_space=pltpu.VMEM), pl.BlockSpec(memory_space=pltpu.SMEM)
-    V = pltpu.VMEM
+    V, S = pltpu.VMEM, pltpu.SemaphoreType.DMA
     return pl.pallas_call(backward_kernel,
-        out_shape=[jax.ShapeDtypeStruct(s, f32) for s in [(T, D), (1, 1), (CHUNKS, 24, W), (24, 256), (24, 128)]],
+        out_shape=[jax.ShapeDtypeStruct(s, f32) for s in [(T, D), (1, 1), (CHUNKS, 24, W)]],
         in_specs=[sm] + [vm] * 7 + [any_] * 14,
-        out_specs=[any_, sm, vm, vm, vm],
+        out_specs=[any_, sm, vm],
         scratch_shapes=[V((T, D), f32), V((D, D), bf16), V((D, FF), bf16), V((FF, D), bf16), V((2, 4, SEQ, SEQ), bf16),
             V((T, D), bf16), V((T, D), f32), V((T, D), bf16), V((T, FF), bf16), V((T, FF), bf16), V((D, T), bf16), V((D, T), bf16),
-            V((T, D), bf16), V((T, 128), bf16), V((128, T), bf16), V((T, 128), f32),
-            V((128, D), f32), V((D, 128), bf16), V((128, D), f32), V((128, FF), f32), V((128, D), f32), V((1, D), f32), V((6, 8, 128), f32), V((4, 8, 128), f32),
-            pltpu.SemaphoreType.DMA((13,)), pltpu.SemaphoreType.DMA((6,)), pltpu.SemaphoreType.DMA((6,)), pltpu.SemaphoreType.DMA((2,)), pltpu.SemaphoreType.DMA(())]
-            + scatter_bufs(CHUNKS, 2, W) + scatter_bufs(1, 1, W) + scatter_bufs(1, 1, 128),
+            V((T, D), bf16), V((T, 128), bf16), V((128, T), bf16), V((T, 128), f32), V((T, 128), f32),
+            V((128, D), f32), V((128, D), bf16), V((128, D), f32), V((128, FF), f32), V((128, D), f32), V((8, 8, 128), f32), V((4, 8, 128), f32),
+            S((13,)), S((10,)), S((10,)), S((2,)), S(())] + scatter_bufs(),
         compiler_params=pltpu.CompilerParams(vmem_limit_bytes=64 << 20, collective_id=1, has_side_effects=True),
-        name="backward")(counts, raw, bits, wup, wdown, g1.reshape(1, D), g2.reshape(1, D), mc, tokens, outgrad, wqkv, wao, win, wout, qkv, e, linv, ctx, hid, mlpin, act, slope)
+        name="backward")(counts, raw, bitsT, wup, wdownT, g1, g2, mc, *arrays)
+
+def finish_kernel(scale, gtok_i, loss_i, wqkv_h, win_h, grads, wdownT, g1, g2,
+                  gtok_o, loss_o, gln1, gwqkv, gwao, gln2, gwin, gwout, gwdown, gwup, wq, wi, wide, held, sem):
+    copy = pltpu.make_async_copy(gtok_i, held, sem.at[0])
+    copy.start()
+    me = lax.axis_index("dp") * lax.axis_size("replica") + lax.axis_index("replica")
+    start = pl.multiple_of((me * 24) // 16 * 16, 16)
+    reads = [pltpu.make_async_copy(h.at[pl.ds(start, 32)], v, sem.at[i]) for i, (h, v) in ((1, (wqkv_h, wq)), (2, (win_h, wi)))]
+    for r in reads: r.start()
+    loss_o[0, 0] = loss_i[0, 0]
+    copy.wait()
+    copy = pltpu.make_async_copy(held, gtok_o, sem.at[0])
+    copy.start()
+    for k in range(12):
+        gwin[:, k * W:(k + 1) * W] = grads[k] * scale
+    for g in range(3):
+        gwao[:, g * W:(g + 1) * W] = grads[13 + 4 * g] * scale
+        for j in range(3):
+            gwqkv[:, j * D + g * W:j * D + (g + 1) * W] = grads[14 + 4 * g + j] * scale
+    widen(wide, wdownT[...].astype(f32))
+    wd = wide[...].astype(bf16)
+    code, other = grads[12, :, :128] * scale, grads[12, :, 128:] * scale
+    lane = lanes_of(24)
+    for j in range(4):
+        v = jnp.where(lane // 32 == j, code, 0.0)
+        hi = v.astype(bf16)
+        lo = (v - hi.astype(f32)).astype(bf16)
+        gwout[24 * j:24 * j + 24, :] = dot(hi, wd) + dot(lo, wd)
+    gwdown[...] = other[:, :BITS]
+    for r in reads: r.wait()
+    odd = me % 2
+    def gain(weights, grad, lane_at, into):
+        w = weights[...].astype(f32)
+        w = jnp.where(odd == 1, w[8:32], w[0:24])
+        return jnp.where(lane == lane_at, jnp.sum(w * grad[...], axis=1, keepdims=True), into)
+    flat = gain(wi, gwin, 65, gain(wq, gwqkv, 64, other))
+    turned = jnp.concatenate([flat, jnp.zeros((104, 128), f32)], axis=0).T
+    gwup[...] = turned[32:32 + BITS, :24]
+    def mine(g):
+        rows = jnp.broadcast_to(g[...].reshape(1, D), (8, D))
+        out = jnp.ones((8, 24), f32)
+        for i in range(32):
+            out = jnp.where(me == i, rows[:, 24 * i:24 * i + 24], out)
+        return out[0:1]
+    gln1[...] = (turned[64:65, :24] / mine(g1))
+    gln2[...] = (turned[65:66, :24] / mine(g2))
+    copy.wait()
+
+def finish(scale, gtok, loss, wqkv, win, grads, wdownT, g1, g2):
+    any_, vm, sm = pl.BlockSpec(memory_space=pl.ANY), pl.BlockSpec(memory_space=pltpu.VMEM), pl.BlockSpec(memory_space=pltpu.SMEM)
+    shapes = [gtok.shape, (1, 1), (1, 24), (24, 3 * D), (24, D), (1, 24), (24, FF), (96, D), (24, BITS), (BITS, 24)]
+    return pl.pallas_call(functools.partial(finish_kernel, scale),
+        out_shape=[jax.ShapeDtypeStruct(s, f32) for s in shapes],
+        in_specs=[any_, sm, any_, any_] + [vm] * 4,
+        out_specs=[any_, sm] + [vm] * 8,
+        scratch_shapes=[pltpu.VMEM((32, 3 * D), bf16), pltpu.VMEM((32, FF), bf16), pltpu.VMEM((128, D), f32), pltpu.VMEM(gtok.shape, f32), pltpu.SemaphoreType.DMA((3,))],
+        name="finish")(gtok, loss, wqkv, win, grads, wdownT, g1, g2)
 
 def kernel_body(tokens, counts, bits, outgrad, g1, wqkv, wao, g2, win, wout, wdown, wup):
-    qkv, e, linv, ctx, hid, mlpin, act, slope, raw, mc = forward(counts, tokens, wqkv, wao, win, wout, g1, g2, wdown)
-    gtok, loss, grads, small, tail = backward(counts, raw, bits, wup, wdown, g1, g2, mc, tokens, outgrad, wqkv, wao, win, wout, qkv, e, linv, ctx, hid, mlpin, act, slope)
-    T = tokens.shape[0]
-    scale = (T * 32) ** -0.5
-    first = (lax.axis_index("dp") * lax.axis_size("replica") + lax.axis_index("replica")) * 2
-    cn = lax.dynamic_slice_in_dim(counts, first, 2)
-    valid = (jnp.arange(SEQ)[None] < cn[:, None]).reshape(T, 1)
-    target = ((2.0 * bits.astype(f32) - 1.0) * BITS ** -0.5).astype(bf16)
-    decoded = jnp.where(valid, jnp.dot(target, wup, preferred_element_type=f32), 0.0)
-    grads = grads * scale
-    small = small * scale
-    gwin = grads[:12].transpose(1, 0, 2).reshape(24, FF)
-    grp = grads[12:].reshape(3, 4, 24, 256)
-    gwao = grp[:, 0].transpose(1, 0, 2).reshape(24, D)
-    gwqkv = grp[:, 1:].transpose(2, 1, 0, 3).reshape(24, 3 * D)
-    G = small[:, :128].reshape(24, 4, 32)[:, :, :BITS].transpose(1, 0, 2).reshape(96, BITS)
-    gwout = jnp.dot(G, wdown.astype(f32).T, precision=lax.Precision.HIGHEST)
-    return (decoded, loss.reshape(()), gtok, tail[:, 0] * scale, gwqkv, gwao, small[:, 128 + 64], gwin, gwout, small[:, 128:128 + BITS], small[:, 160:160 + BITS].T)
-
+    bitsT, wdownT = bits.T, wdown.T
+    qkv, e, linv, ctx, hid, mlpin, act, slope, decoded, raw, mc = forward(counts, tokens, wqkv, wao, win, wout, g1, g2, wdownT, bitsT, wup)
+    gtok, loss, grads = backward(counts, raw, bitsT, wup, wdownT, g1, g2, mc, tokens, outgrad, wqkv, wao, win, wout, qkv, e, linv, ctx, hid, mlpin, act, slope)
+    scale = (tokens.shape[0] * lax.axis_size(("dp", "replica"))) ** -0.5
+    gtok, loss, gln1, gwqkv, gwao, gln2, gwin, gwout, gwdown, gwup = finish(scale, gtok, loss, wqkv, win, grads, wdownT, g1, g2)
+    return (decoded, loss.reshape(()), gtok, gln1.reshape(24), gwqkv, gwao, gln2.reshape(24), gwin, gwout, gwdown, gwup)
 
 eps_norm = 1e-06
 neg_big = -1e30

time: 182 us -> 169 us (0.929)
  local copies, waits for them, and re-layouts: 10.6 us -> 0 us
  Pallas kernels: 162 us -> 168 us
  other arithmetic: 3.35 us -> 0 us
  matrix products: 2.97 us -> 0 us
    pallas_call x0 -> x1, Pallas kernels: none -> 6.99 us  [finish(): pl.pallas_call(functools.partial(finish_kernel, scale), out_shape=[jax.Sh...]
    unnamed x21 -> x0, local copies, waits for them, and re-layouts: 5.62 us -> none
    reshape x6 -> x0, local copies, waits for them, and re-layouts: 4.28 us -> none  [the longest x1 1.27 us: forward(): g2.reshape(1, D)]
    dot_general x2 -> x0, matrix products: 2.97 us -> none  [the longest x1 1.92 us: kernel_body(): jnp.dot(target, wup, preferred_element_type=f32)]
    mul x2 -> x0, other arithmetic: 1.86 us -> none  [the longest x1 1.12 us: kernel_body(): grads = grads * scale]
where the time goes in v2:
time: 169 us
  Pallas kernels  168 us (99%)
    pallas_call x1, Pallas kernels, backward(): pl.pallas_call(backward_kernel, out_shape=[jax.ShapeDtypeStruct(s, f32) f...  127 us
    pallas_call x1, Pallas kernels, forward(): pl.pallas_call(forward_kernel, out_shape=[jax.ShapeDtypeStruct(*o) for o...  33.3 us
    pallas_call x1, Pallas kernels, finish(): pl.pallas_call(functools.partial(finish_kernel, scale), out_shape=[jax.Sh...  6.99 us

profile of v2, /device:TPU:0, one launch (start us, length us, event | category | flops | bytes accessed | tf_op | source)
XLA Modules:
  0.0 168.5 jit_solution(15457893136882676458)
XLA Ops:
  0.6 33.3 %forward.1 = (bf16[2304,768]{1,0:T(8,128)(2,1)}, bf16[24,384,384]{2,1,0:T(8,128)(2,1)}, f32[768,768]{1,0:T(8,128)}, bf16[768,768]{1,0:T(8,128)(2,1)}, f32[768,76...) custom-call(s32[64]{0:T(128)} %counts.3, ...), custom_call_target="tpu_custom_call" | custom-call | tf_op jit(solution)/shard_map/forward/pallas_call | solution.py:147
  33.9 127.5 %backward.1 = (f32[768,768]{1,0:T(8,128)}, f32[1,1]{1,0:T(1,128)}, f32[25,24,256]{2,1,0:T(8,128)}) custom-call(s32[64]{0:T(128)} %counts.3, f32[768,128]{1,0:T(8,128)} %get-tuple-element.36.raw, s32[18,768]{1,0:T(8,128)} %bitcast.9, bf16[18,768]{1,0:T(8,128)(2,1)} %wup.3, bf16[18,768]{1,0:T(8,128)(2,1)} %bitcast.6, f32[768]{0:T(1024)} %g1.5, f32[768]{0:T(1024)} %g2.5, ...), custom_call_target="tpu_custom_call" | custom-call | tf_op jit(solution)/shard_map/backward/pallas_call | solution.py:499
  161.4 7.0 %finish.1 = (f32[768,768]{1,0:T(8,128)}, f32[1,1]{1,0:T(1,128)}, f32[1,24]{1,0:T(1,128)}, f32[24,2304]{1,0:T(8,128)}, f32[24,768]{1,0:T(8,128)}, /*index=5*/f32[...) custom-call(f32[768,768]{1,0:T(8,128)} %get-tuple-element.46.gtok_i, ...), custom_call_target="tpu_custom_call" | custom-call | tf_op jit(solution)/shard_map/finish/pallas_call | solution.py:561

commit v3 on v2

--- a/solution.py
+++ b/solution.py
@@ -39,124 +39,10 @@
     pdf = jnp.exp(x * x * -0.5) * (1.0 / math.sqrt(2.0 * math.pi))
     return x * cdf, cdf + x * pdf
 
-MC = 512
-def forward_kernel(counts, tokens_h, wqkv_h, wao_h, win_h, wout_h, g1, g2, wdownT, bitsT, wup,
-                   qkv_h, e_h, linv_h, ctx_h, hid_h, mlpin_h, act_h, slope_h, dec_h, raw_o, mc_o,
-                   tokens, wqkv, wao, win, wout, attn_in, qkv, e, linv, ctx, hid, mlpin, act, slope, dec, wide, wd4, sem, osem):
-    loads = [pltpu.make_async_copy(s, d, sem.at[i]) for i, (s, d) in enumerate(
-        [(tokens_h, tokens), (wqkv_h, wqkv), (wao_h, wao), (wout_h, wout), (win_h, win)])]
-    for l in loads: l.start()
-    outs = []
-    def put(src, dst):
-        cp = pltpu.make_async_copy(src, dst, osem.at[len(outs)])
-        cp.start(); outs.append(cp)
-    first = (lax.axis_index("dp") * lax.axis_size("replica") + lax.axis_index("replica")) * 2
-    n0, n1 = counts[first], counts[first + 1]
-    widen(wide, wup[...].astype(f32))
-    up = wide[...].astype(bf16)
-    widen(wide, (2.0 * bitsT[...].astype(f32) - 1.0) * BITS ** -0.5)
-    wide_t = (wide[...].T * 0.25).astype(bf16)
-    for i in range(3):
-        r = pl.ds(i * 256, 256)
-        row = lax.broadcasted_iota(jnp.int32, (256, D), 0) + i * 256
-        live = row < jnp.where(row < SEQ, n0, n1 + SEQ)
-        dec[r, :] = jnp.where(live, dot(wide_t[i * 256:(i + 1) * 256], up), 0.0)
-    put(dec, dec_h)
-    widen(wide, wdownT[...].astype(f32))
-    wd4[...] = wide[...].T.astype(bf16)
-    loads[0].wait()
-    def ln1(i, _):
-        r = cols(i, 128)
-        n, _inv = norm_stats(tokens[r, :])
-        attn_in[r, :] = (n * g1[...].reshape(1, D)).astype(bf16)
-        return 0
-    lax.fori_loop(0, 6, ln1, 0)
-    loads[1].wait()
-    def proj(i, _):
-        v = dot(attn_in[...], wqkv[:, cols(i, 256)])
-        v = v * jnp.where(i < 3, 0.125, 1.0)
-        qkv[pl.ds(pl.multiple_of(i // 3 * D, D), D), cols(i % 3, 256)] = v.astype(bf16)
-        return 0
-    lax.fori_loop(0, 9, proj, 0)
-    put(qkv, qkv_h)
-    def att(i, _):
-        img = i // 3
-        n = jnp.where(img == 0, n0, n1)
-        r = pl.ds(pl.multiple_of(img * SEQ, SEQ), SEQ)
-        ok = lax.broadcasted_iota(jnp.int32, (1, SEQ), 1) < n
-        low = lanes_of(SEQ) < HEAD
-        one = jnp.ones((SEQ, 128), bf16)
-        for j in range(2):
-            o = i % 3 * 2 + j
-            q2, k2, v2 = (qkv[pl.ds(pl.multiple_of(b * D + img * SEQ, 128), SEQ), cols(o, 128)] for b in range(3))
-            zero = jnp.zeros_like(q2)
-            vo = jnp.concatenate([v2, one], axis=1)
-            res = []
-            for h in range(2):
-                q = jnp.where(low, q2, zero) if h == 0 else jnp.where(low, zero, q2)
-                s = jnp.where(ok, dot(q, k2, 1, 1), -1e30)
-                m = jnp.max(s, axis=1, keepdims=True)
-                p = jnp.exp(s - m).astype(bf16)
-                e[img * HEADS + o * 2 + h] = p
-                ov = dot(p, vo)
-                inv = 1.0 / ov[:, 128:]
-                res.append((ov[:, :128] * inv, inv))
-            cs = pl.ds(pl.multiple_of(o * 128, 128), 128)
-            ctx[r, cs] = jnp.where(low, res[0][0], res[1][0]).astype(bf16)
-            linv[r, cs] = jnp.where(low, res[0][1], res[1][1])
-        return 0
-    lax.fori_loop(0, 6, att, 0)
-    put(e, e_h); put(linv, linv_h); put(ctx, ctx_h)
-    loads[2].wait()
-    def ao(i, _):
-        r = cols(i, 256)
-        h = tokens[r, :] + dot(ctx[r, :], wao[...])
-        hid[r, :] = h
-        n, _inv = norm_stats(h)
-        mlpin[r, :] = (n * g2[...].reshape(1, D)).astype(bf16)
-        return 0
-    lax.fori_loop(0, 3, ao, 0)
-    put(hid, hid_h); put(mlpin, mlpin_h)
-    loads[3].wait()
-    def mcf(i, _):
-        r = cols(i, 768)
-        v = dot(wout[r, :], wd4[...])
-        hi = v.astype(bf16).astype(f32)
-        mc_o[r, :] = jnp.where(lanes_of(768) % 64 < 32, hi, v - hi).astype(bf16)
-        return 0
-    lax.fori_loop(0, 4, mcf, 0)
-    loads[4].wait()
-    def mlp(i, _):
-        cs = cols(i, MC)
-        a, s = gelu_parts(dot(mlpin[...], win[:, cs]))
-        act[:, cs] = a.astype(bf16)
-        slope[:, cs] = s.astype(bf16)
-        return 0
-    lax.fori_loop(0, FF // MC, mlp, 0)
-    put(act, act_h); put(slope, slope_h)
-    raw = dot(act[...], mc_o[...])
-    raw = raw + pltpu.roll(raw, 32, 1)
-    raw_o[...] = raw + dot(hid[...].astype(bf16), wd4[...])
-    for o in outs: o.wait()
-
-def forward(counts, tokens, wqkv, wao, win, wout, g1, g2, wdownT, bitsT, wup):
-    T = tokens.shape[0]
-    any_, vm = pl.BlockSpec(memory_space=pl.ANY), pl.BlockSpec(memory_space=pltpu.VMEM)
-    outs = [((3 * D, D), bf16), ((24, SEQ, SEQ), bf16), ((T, D), f32), ((T, D), bf16), ((T, D), f32), ((T, D), bf16),
-            ((T, FF), bf16), ((T, FF), bf16), ((T, D), f32)]
-    return pl.pallas_call(forward_kernel,
-        out_shape=[jax.ShapeDtypeStruct(*o) for o in outs] + [jax.ShapeDtypeStruct((T, 128), f32), jax.ShapeDtypeStruct((FF, 128), bf16)],
-        in_specs=[pl.BlockSpec(memory_space=pltpu.SMEM)] + [any_] * 5 + [vm] * 5,
-        out_specs=[any_] * 9 + [vm] * 2,
-        scratch_shapes=[pltpu.VMEM((T, D), f32), pltpu.VMEM((D, 3 * D), bf16), pltpu.VMEM((D, D), bf16), pltpu.VMEM((D, FF), bf16), pltpu.VMEM((FF, D), bf16),
-            pltpu.VMEM((T, D), bf16)] + [pltpu.VMEM(*o) for o in outs] + [pltpu.VMEM((128, D), f32), pltpu.VMEM((D, 128), bf16), pltpu.SemaphoreType.DMA((5,)), pltpu.SemaphoreType.DMA((9,))],
-        compiler_params=pltpu.CompilerParams(vmem_limit_bytes=63 << 20),
-        name="forward")(counts, tokens, wqkv, wao, win, wout, g1, g2, wdownT, bitsT, wup)
-
 MESH = pl.DeviceIdType.MESH
 W = 256
 CHUNKS = 25
-LAGS = (0, 1, 5, 7, 9, 10)
+LAGS = (0, 1, 6, 10, 13, 16)
 
 def place():
     dp, rp = lax.axis_index("dp"), lax.axis_index("replica")
@@ -174,17 +60,17 @@
     z, x, y, c = place()
     return [device((z + d) % 4, x, y, c) for d in (1, 2, 3)]
 
-def enter():
-    bar = pltpu.get_barrier_semaphore()
-    peers = near() + column()
-    for p in peers:
-        pl.semaphore_signal(bar, inc=1, device_id=p, device_id_type=MESH)
-    pl.semaphore_wait(bar, len(peers))
+def arrive():
+    for p in near() + column():
+        pl.semaphore_signal(pltpu.get_barrier_semaphore(), inc=1, device_id=p, device_id_type=MESH)
+
+def all_arrived():
+    pl.semaphore_wait(pltpu.get_barrier_semaphore(), len(near() + column()))
 
 def planar(k):
     if isinstance(k, int):
-        return int(k % 4 == 0 if k <= 12 else k % 2 == 1)
-    return jnp.where(k <= 12, jnp.where(lax.rem(k, 4) == 0, 1, 0), lax.rem(k, 2))
+        return int((k % 3 if k <= 12 else (k + 3) % 4) == 0)
+    return jnp.where(jnp.where(k <= 12, lax.rem(k, 3), lax.rem(k + 3, 4)) == 0, 1, 0)
 
 class Scatter:
     def __init__(self, bufs, result):
@@ -272,35 +158,123 @@
     return inv * (gn - mean - normed * spread)
 
 RB = 128
-def backward_kernel(counts, raw, bitsT, wup, wdownT, g1, g2, mc,
-                    tokens_h, outgrad_h, wqkv_h, wao_h, win_h, wout_h, qkv_h, e_h, linv_h, ctx_h, hid_h, mlpin_h, act_h, slope_h,
-                    gtok_h, loss_o, grads_o,
-                    big, wao, win, wout, e, ctx, hid, mlpin, act, slope, mlpinT, ainT, dattn, draw, drawT, unit_s, target,
-                    wide, wd4t, smallT, gT, quantT, s8, zs, sem, ssem, rsem, esem, osem, *bufs):
+MC = 512
+def train_kernel(counts, bitsT, wup, wdownT, g1, g2, tokens_h, outgrad_h, wqkv_h, wao_h, win_h, wout_h,
+                 gtok_h, loss_o, grads_o, qkv_h, e_h, linv_h,
+                 hid, big, win, wout, wao, e, ctx, mlpin, act, slope, mlpinT, ainT, dattn, draw, drawT, unit_s, target, raw, mc,
+                 wide, wd4t, smallT, quantT, s8, zs, sem, osem, ssem, rsem, esem, *bufs):
     def result(k, h, v):
         grads_o[k, :, h * 128:(h + 1) * 128] = v
     main = Scatter(bufs, result)
     z, x, y, c = place()
-    names = dict(outgrad=(outgrad_h, big), mlpin=(mlpin_h, mlpin), slope=(slope_h, slope), act=(act_h, act), hid=(hid_h, hid),
-                 wout=(wout_h, wout), win=(win_h, win), ctx=(ctx_h, ctx), wao=(wao_h, wao), qkv=(qkv_h, wout.at[:3 * D]),
-                 linv=(linv_h, big), wqkv=(wqkv_h, win.at[:, :3 * D]), tokens=(tokens_h, big))
-    order = list(names)
-    loads = {n: pltpu.make_async_copy(*names[n], sem.at[i]) for i, n in enumerate(order)}
-    for n in order[:9]:
-        loads[n].start()
+    loads = {n: pltpu.make_async_copy(src, dst, sem.at[i]) for i, (n, src, dst) in enumerate((
+        ("tokens", tokens_h, hid), ("wqkv", wqkv_h, win.at[:, :3 * D]), ("wao", wao_h, wao), ("win", win_h, win), ("wout", wout_h, wout),
+        ("outgrad", outgrad_h, big), ("qkv", qkv_h, wout.at[:3 * D]), ("linv", linv_h, big), ("wqkv2", wqkv_h, win.at[:, :3 * D]), ("tokens2", tokens_h, big)))}
+    saves = {n: pltpu.make_async_copy(src, dst, osem.at[i]) for i, (n, src, dst) in enumerate((
+        ("qkv", wout.at[:3 * D], qkv_h), ("linv", big, linv_h), ("gtok", hid, gtok_h)))}
     def load_e(g, img):
         return pltpu.make_async_copy(e_h.at[pl.ds(img * HEADS + g * 4, 4)], e.at[img], esem.at[img])
-    for img in range(2):
-        load_e(0, img).start()
-    enter()
+    def save_e(g, img):
+        return pltpu.make_async_copy(e.at[img], e_h.at[pl.ds(img * HEADS + g * 4, 4)], esem.at[2 + img])
+    arrive()
+    for n in ("tokens", "wqkv", "wao"):
+        loads[n].start()
     first = (lax.axis_index("dp") * lax.axis_size("replica") + lax.axis_index("replica")) * 2
     n0, n1 = counts[first], counts[first + 1]
     total = lax.fori_loop(0, counts.shape[0], lambda i, a: a + counts[i], jnp.int32(0)).astype(f32)
-    widen(wide, (2.0 * bitsT[...].astype(f32) - 1.0) * BITS ** -0.5)
-    target[...] = wide[...].T
     def live(i):
         row = lax.broadcasted_iota(jnp.int32, (RB, 128), 0) + i * RB
         return row < jnp.where(row < SEQ, n0, n1 + SEQ)
+    low = lanes_of(SEQ) < HEAD
+    widen(wide, wdownT[...].astype(f32))
+    wd4t[...] = wide[...].astype(bf16)
+    widen(wide, (2.0 * bitsT[...].astype(f32) - 1.0) * BITS ** -0.5)
+    target[...] = wide[...].T
+    loads["tokens"].wait()
+    def fwd_ln1(i, _):
+        r = cols(i, 128)
+        n, _inv = norm_stats(hid[r, :])
+        dattn[r, :] = (n * g1[...].reshape(1, D)).astype(bf16)
+        return 0
+    lax.fori_loop(0, 6, fwd_ln1, 0)
+    loads["wqkv"].wait()
+    def proj(i, _):
+        v = dot(dattn[...], win[:, cols(i, 256)])
+        v = v * jnp.where(i < 3, 0.125, 1.0)
+        wout[pl.ds(pl.multiple_of(i // 3 * D, D), D), cols(i % 3, 256)] = v.astype(bf16)
+        return 0
+    lax.fori_loop(0, 9, proj, 0)
+    loads["win"].start()
+    saves["qkv"].start()
+    def heads_of(img, o):
+        return (wout[pl.ds(pl.multiple_of(b * D + img * SEQ, 128), SEQ), cols(o, 128)] for b in range(3))
+    def att(g, _):
+        def image(img, _):
+            n = jnp.where(img == 0, n0, n1)
+            r = pl.ds(pl.multiple_of(img * SEQ, SEQ), SEQ)
+            ok = lax.broadcasted_iota(jnp.int32, (1, SEQ), 1) < n
+            one = jnp.ones((SEQ, 128), bf16)
+            @pl.when(g > 0)
+            def _():
+                save_e(g - 1, img).wait()
+            for j in range(2):
+                o = g * 2 + j
+                q2, k2, v2 = heads_of(img, o)
+                zero = jnp.zeros_like(q2)
+                vo = jnp.concatenate([v2, one], axis=1)
+                res = []
+                for h in range(2):
+                    q = jnp.where(low, q2, zero) if h == 0 else jnp.where(low, zero, q2)
+                    s = jnp.where(ok, dot(q, k2, 1, 1), -1e30)
+                    m = jnp.max(s, axis=1, keepdims=True)
+                    p = jnp.exp(s - m).astype(bf16)
+                    e[img, 2 * j + h] = p
+                    ov = dot(p, vo)
+                    inv = 1.0 / ov[:, 128:]
+                    res.append((ov[:, :128] * inv, inv))
+                ctx[r, cols(o, 128)] = jnp.where(low, res[0][0], res[1][0]).astype(bf16)
+                big[r, cols(o, 128)] = jnp.where(low, res[0][1], res[1][1])
+            save_e(g, img).start()
+            return 0
+        lax.fori_loop(0, 2, image, 0)
+        return 0
+    lax.fori_loop(0, 3, att, 0)
+    saves["linv"].start()
+    saves["qkv"].wait()
+    loads["wout"].start()
+    loads["wao"].wait()
+    def ao(i, _):
+        r = cols(i, 256)
+        h = hid[r, :] + dot(ctx[r, :], wao[...])
+        hid[r, :] = h
+        n, _inv = norm_stats(h)
+        mlpin[r, :] = (n * g2[...].reshape(1, D)).astype(bf16)
+        return 0
+    lax.fori_loop(0, 3, ao, 0)
+    saves["linv"].wait()
+    loads["outgrad"].start()
+    loads["wout"].wait()
+    def mcf(i, _):
+        r = cols(i, 768)
+        v = dot(wout[r, :], wd4t[...], 1, 1)
+        hi = v.astype(bf16).astype(f32)
+        mc[r, :] = jnp.where(lanes_of(768) % 64 < 32, hi, v - hi).astype(bf16)
+        return 0
+    lax.fori_loop(0, 4, mcf, 0)
+    loads["win"].wait()
+    for img in range(2):
+        save_e(2, img).wait()
+        load_e(0, img).start()
+    def fwd_mlp(i, _):
+        cs = cols(i, MC)
+        a, s = gelu_parts(dot(mlpin[...], win[:, cs]))
+        act[:, cs] = a.astype(bf16)
+        slope[:, cs] = s.astype(bf16)
+        return 0
+    lax.fori_loop(0, FF // MC, fwd_mlp, 0)
+    rawv = dot(act[...], mc[...])
+    raw[...] = rawv + pltpu.roll(rawv, 32, 1) + dot(hid[...].astype(bf16), wd4t[...], 1, 1)
+    all_arrived()
     def codes(i):
         r = cols(i, RB)
         rawv = raw[r, :]
@@ -331,7 +305,7 @@
             dattn[r, cs] = jnp.where(ok, big[r, cs], 0.0).astype(bf16)
         return 0
     lax.fori_loop(0, 768 // RB, decode, 0)
-    quantT[...] = dot(wide[...].astype(bf16), dattn[...])
+    quantT[...] = dot(target[...].astype(bf16), dattn[...], 0, 0)
     for t in tells: t.wait_recv()
     s = s8[0]
     for i in range(1, 8):
@@ -342,10 +316,7 @@
     for t in tells: t.wait_send()
     widen(wide, wup[...].astype(f32))
     unit_s[...] = dot(dattn[...], wide[...].astype(bf16), 1, 1)
-    loads["mlpin"].wait()
     mlpinT[...] = mlpin[...].T
-    widen(wide, wdownT[...].astype(f32))
-    wd4t[...] = wide[...].astype(bf16)
     for t in ztells: t.wait()
     zsum = zs[0] + zs[1] + zs[2] + zs[3]
     bit8 = lanes_of(8) % 32 < BITS
@@ -364,13 +335,12 @@
         draw[r, :] = graw.astype(bf16)
         return 0
     lax.fori_loop(0, 768 // RB, unit_back, 0)
-    loads["slope"].wait()
     def put(t, p, v):
         for h in range(2):
             main.put(t % 2, p, v[:, h * 128:(h + 1) * 128], h)
     def mlp(i, _):
-        for j in range(4):
-            t = 4 * i + j
+        for j in range(6):
+            t = 6 * i + j
             cs = cols(t, W)
             d = dot(draw[...], mc[cs, :], 1, 1) * 0.5
             dp = (slope[:, cs].astype(f32) * d).astype(bf16)
@@ -379,32 +349,32 @@
             put(j, planar(j), dot(mlpinT[...], dp))
             main.early(t, j % 2)
         return 0
-    lax.fori_loop(0, 3, mlp, 0)
+    lax.fori_loop(0, 2, mlp, 0)
     main.late(12)
     drawT[...] = draw[...].T
-    loads["act"].wait()
-    gT[...] = dot(drawT[...], act[...])
+    for q in range(4):
+        big[128 * q:128 * q + 128, :] = dot(drawT[...], act[:, q * D:(q + 1) * D])
     for b in range(8):
-        t = gT[:, b * 384:(b + 1) * 384].T.reshape(4, 4, 24, 128)
+        t = big[b // 2 * 128:b // 2 * 128 + 128, b % 2 * 384:b % 2 * 384 + 384].T.reshape(4, 4, 24, 128)
         l4 = lax.broadcasted_iota(jnp.int32, (4, 24, 128), 2) // 32
         s = jnp.where(l4 == 0, t[:, 0], 0.0)
         for j in range(1, 4):
             s = jnp.where(l4 == j, t[:, j], s)
         unit_s[b * 96:(b + 1) * 96, :] = s.reshape(96, 128)
     main.put(0, 1, unit_s[...], 0)
-    loads["hid"].wait()
-    loads["wout"].wait()
-    gv = gT[...]
-    hi = gv.astype(bf16)
-    lo = (gv - hi.astype(f32)).astype(bf16)
-    gwd = dot(drawT[...], hid[...].astype(bf16)) + dot(hi, wout[...]) + dot(lo, wout[...])
+    gwd = dot(drawT[...], hid[...].astype(bf16))
+    for q in range(4):
+        gv = big[128 * q:128 * q + 128, :]
+        hi = gv.astype(bf16)
+        lo = (gv - hi.astype(f32)).astype(bf16)
+        w = wout[q * D:(q + 1) * D, :]
+        gwd = gwd + (dot(hi, w) + dot(lo, w))
     r128 = lax.broadcasted_iota(jnp.int32, (128, D), 0)
     smallT[...] = jnp.where(r128 < 32, gwd, quantT[...])
     for i in range(6):
         unit_s[i * 128:(i + 1) * 128, :] = smallT[:, i * 128:(i + 1) * 128].T
     main.put(0, 1, unit_s[...], 1)
     main.early(12, 0)
-    loads["win"].wait()
     loads["linv"].start()
     loads["qkv"].start()
     main.late(13)
@@ -417,10 +387,7 @@
         dattn[r, :] = v.astype(bf16)
         return 0
     lax.fori_loop(0, 3, ln2, 0)
-    loads["wqkv"].start()
-    main.late(14)
-    loads["ctx"].wait()
-    loads["wao"].wait()
+    loads["wqkv2"].start()
     loads["linv"].wait()
     mlpinT[...] = ctx[...].T
     def dctx(i, _):
@@ -428,17 +395,16 @@
         mlpin[r, :] = (dot(dattn[r, :], wao[...], 1, 1) * big[r, :]).astype(bf16)
         return 0
     lax.fori_loop(0, 3, dctx, 0)
-    loads["tokens"].start()
+    loads["tokens2"].start()
     loads["qkv"].wait()
-    low = lanes_of(SEQ) < HEAD
-    loads["tokens"].wait()
+    loads["tokens2"].wait()
     for i in range(6):
         r = pl.ds(i * 128, 128)
         nrm, inv = norm_stats(big[r, :])
         ainT[:, i * 128:(i + 1) * 128] = (nrm * g1[...].reshape(1, D)).astype(bf16).T
     def group(g, _):
         t0 = 13 + 4 * g
-        main.late(t0 + 2)
+        main.late(t0 + 1)
         put(1, 1, dot(mlpinT[...], dattn[:, cols(g, W)]))
         main.early(t0, 1)
         def image(img, _):
@@ -446,8 +412,8 @@
             r = pl.ds(pl.multiple_of(img * SEQ, SEQ), SEQ)
             for j in range(2):
                 o = g * 2 + j
-                q2, k2, v2 = (wout[pl.ds(pl.multiple_of(b * D + img * SEQ, 128), SEQ), cols(o, 128)] for b in range(3))
-                cs = pl.ds(pl.multiple_of(o * 128, 128), 128)
+                q2, k2, v2 = heads_of(img, o)
+                cs = cols(o, 128)
                 d2, c2 = mlpin[r, cs], ctx[r, cs]
                 prod = d2.astype(f32) * c2.astype(f32)
                 zero_ = jnp.zeros_like(q2)
@@ -466,19 +432,19 @@
             @pl.when(g < 2)
             def _():
                 load_e(g + 1, img).start()
-            main.late(t0 + 3 + img)
+            main.late(t0 + 2 + img)
             return 0
         lax.fori_loop(0, 2, image, 0)
         for j in range(3):
-            put(j, j % 2, dot(ainT[...], act[:, pl.ds(pl.multiple_of(j * D + g * W, W), W)]))
+            put(j, 0, dot(ainT[...], act[:, pl.ds(pl.multiple_of(j * D + g * W, W), W)]))
             main.early(t0 + 1 + j, j % 2)
             if j == 1:
-                main.late(t0 + 5)
+                main.late(t0 + 4)
         return 0
     lax.fori_loop(0, 3, group, 0)
     main.early(25, 1)
-    main.late(27)
-    loads["wqkv"].wait()
+    main.late(26)
+    loads["wqkv2"].wait()
     def ln1(i, _):
         r = cols(i, 256)
         dn = dot(act[r, :3 * D], win[:, :3 * D], 1, 1)
@@ -486,40 +452,54 @@
         hid[r, :] += norm_back(dn, nrm, inv, g1[...].reshape(1, D))
         return 0
     lax.fori_loop(0, 3, ln1, 0)
-    gtok = pltpu.make_async_copy(hid, gtok_h, osem)
-    gtok.start()
-    for t in range(28, CHUNKS + LAGS[5]):
+    saves["gtok"].start()
+    for t in range(27, CHUNKS + LAGS[5]):
         main.late(t)
-    gtok.wait()
-
-def backward(counts, raw, bitsT, wup, wdownT, g1, g2, mc, *arrays):
+    saves["gtok"].wait()
+
+def train(*args):
     T = 768
     any_, vm, sm = pl.BlockSpec(memory_space=pl.ANY), pl.BlockSpec(memory_space=pltpu.VMEM), pl.BlockSpec(memory_space=pltpu.SMEM)
     V, S = pltpu.VMEM, pltpu.SemaphoreType.DMA
-    return pl.pallas_call(backward_kernel,
-        out_shape=[jax.ShapeDtypeStruct(s, f32) for s in [(T, D), (1, 1), (CHUNKS, 24, W)]],
-        in_specs=[sm] + [vm] * 7 + [any_] * 14,
-        out_specs=[any_, sm, vm],
-        scratch_shapes=[V((T, D), f32), V((D, D), bf16), V((D, FF), bf16), V((FF, D), bf16), V((2, 4, SEQ, SEQ), bf16),
-            V((T, D), bf16), V((T, D), f32), V((T, D), bf16), V((T, FF), bf16), V((T, FF), bf16), V((D, T), bf16), V((D, T), bf16),
-            V((T, D), bf16), V((T, 128), bf16), V((128, T), bf16), V((T, 128), f32), V((T, 128), f32),
-            V((128, D), f32), V((128, D), bf16), V((128, D), f32), V((128, FF), f32), V((128, D), f32), V((8, 8, 128), f32), V((4, 8, 128), f32),
-            S((13,)), S((10,)), S((10,)), S((2,)), S(())] + scatter_bufs(),
+    shapes = [((T, D), f32), ((1, 1), f32), ((CHUNKS, 24, W), f32), ((3 * T, D), bf16), ((24, SEQ, SEQ), bf16), ((T, D), f32)]
+    return pl.pallas_call(train_kernel,
+        out_shape=[jax.ShapeDtypeStruct(*s) for s in shapes],
+        in_specs=[sm] + [vm] * 5 + [any_] * 6,
+        out_specs=[any_, sm, vm] + [any_] * 3,
+        scratch_shapes=[V((T, D), f32), V((T, D), f32), V((D, FF), bf16), V((FF, D), bf16), V((D, D), bf16), V((2, 4, SEQ, SEQ), bf16),
+            V((T, D), bf16), V((T, D), bf16), V((T, FF), bf16), V((T, FF), bf16), V((D, T), bf16), V((D, T), bf16), V((T, D), bf16),
+            V((T, 128), bf16), V((128, T), bf16), V((T, 128), f32), V((T, 128), f32), V((T, 128), f32), V((FF, 128), bf16),
+            V((128, D), f32), V((128, D), bf16), V((128, D), f32), V((128, D), f32), V((8, 8, 128), f32), V((4, 8, 128), f32),
+            S((10,)), S((3,)), S((10,)), S((10,)), S((4,))] + scatter_bufs(),
         compiler_params=pltpu.CompilerParams(vmem_limit_bytes=64 << 20, collective_id=1, has_side_effects=True),
-        name="backward")(counts, raw, bitsT, wup, wdownT, g1, g2, mc, *arrays)
-
-def finish_kernel(scale, gtok_i, loss_i, wqkv_h, win_h, grads, wdownT, g1, g2,
-                  gtok_o, loss_o, gln1, gwqkv, gwao, gln2, gwin, gwout, gwdown, gwup, wq, wi, wide, held, sem):
-    copy = pltpu.make_async_copy(gtok_i, held, sem.at[0])
-    copy.start()
+        name="train")(*args)
+
+PIECES = 4
+def finish_kernel(scale, counts, gtok_i, loss_i, wqkv_h, win_h, grads, wdownT, g1, g2, bitsT, wup,
+                  dec_h, gtok_o, loss_o, gln1, gwqkv, gwao, gln2, gwin, gwout, gwdown, gwup, wq, wi, wide, held, dec, sem, csem):
+    part = lambda i: pl.ds(i * (768 // PIECES), 768 // PIECES)
+    take = [pltpu.make_async_copy(gtok_i.at[part(i)], held.at[part(i)], csem.at[0, i]) for i in range(PIECES)]
+    give = [pltpu.make_async_copy(held.at[part(i)], gtok_o.at[part(i)], csem.at[1, i]) for i in range(PIECES)]
+    show = [pltpu.make_async_copy(dec.at[part(i)], dec_h.at[part(i)], csem.at[2, i]) for i in range(PIECES)]
+    for t in take: t.start()
     me = lax.axis_index("dp") * lax.axis_size("replica") + lax.axis_index("replica")
     start = pl.multiple_of((me * 24) // 16 * 16, 16)
-    reads = [pltpu.make_async_copy(h.at[pl.ds(start, 32)], v, sem.at[i]) for i, (h, v) in ((1, (wqkv_h, wq)), (2, (win_h, wi)))]
+    reads = [pltpu.make_async_copy(h.at[pl.ds(start, 32)], v, sem.at[i]) for i, (h, v) in ((0, (wqkv_h, wq)), (1, (win_h, wi)))]
     for r in reads: r.start()
     loss_o[0, 0] = loss_i[0, 0]
-    copy.wait()
-    copy = pltpu.make_async_copy(held, gtok_o, sem.at[0])
-    copy.start()
+    n0, n1 = counts[2 * me], counts[2 * me + 1]
+    widen(wide, wup[...].astype(f32))
+    up = wide[...].astype(bf16)
+    widen(wide, (2.0 * bitsT[...].astype(f32) - 1.0) * BITS ** -0.5)
+    target = (wide[...].T * 0.25).astype(bf16)
+    rows = 768 // PIECES
+    for i in range(PIECES):
+        row = lax.broadcasted_iota(jnp.int32, (rows, D), 0) + i * rows
+        live = row < jnp.where(row < SEQ, n0, n1 + SEQ)
+        dec[part(i), :] = jnp.where(live, dot(target[i * rows:(i + 1) * rows], up), 0.0)
+        show[i].start()
+        take[i].wait()
+        give[i].start()
     for k in range(12):
         gwin[:, k * W:(k + 1) * W] = grads[k] * scale
     for g in range(3):
@@ -553,24 +533,24 @@
         return out[0:1]
     gln1[...] = (turned[64:65, :24] / mine(g1))
     gln2[...] = (turned[65:66, :24] / mine(g2))
-    copy.wait()
-
-def finish(scale, gtok, loss, wqkv, win, grads, wdownT, g1, g2):
+    for t in give + show: t.wait()
+
+def finish(scale, counts, gtok, *rest):
     any_, vm, sm = pl.BlockSpec(memory_space=pl.ANY), pl.BlockSpec(memory_space=pltpu.VMEM), pl.BlockSpec(memory_space=pltpu.SMEM)
-    shapes = [gtok.shape, (1, 1), (1, 24), (24, 3 * D), (24, D), (1, 24), (24, FF), (96, D), (24, BITS), (BITS, 24)]
+    shapes = [gtok.shape, gtok.shape, (1, 1), (1, 24), (24, 3 * D), (24, D), (1, 24), (24, FF), (96, D), (24, BITS), (BITS, 24)]
     return pl.pallas_call(functools.partial(finish_kernel, scale),
         out_shape=[jax.ShapeDtypeStruct(s, f32) for s in shapes],
-        in_specs=[any_, sm, any_, any_] + [vm] * 4,
-        out_specs=[any_, sm] + [vm] * 8,
-        scratch_shapes=[pltpu.VMEM((32, 3 * D), bf16), pltpu.VMEM((32, FF), bf16), pltpu.VMEM((128, D), f32), pltpu.VMEM(gtok.shape, f32), pltpu.SemaphoreType.DMA((3,))],
-        name="finish")(gtok, loss, wqkv, win, grads, wdownT, g1, g2)
+        in_specs=[sm, any_, sm, any_, any_] + [vm] * 6,
+        out_specs=[any_, any_, sm] + [vm] * 8,
+        scratch_shapes=[pltpu.VMEM((32, 3 * D), bf16), pltpu.VMEM((32, FF), bf16), pltpu.VMEM((128, D), f32), pltpu.VMEM(gtok.shape, f32), pltpu.VMEM(gtok.shape, f32),
+            pltpu.SemaphoreType.DMA((2,)), pltpu.SemaphoreType.DMA((3, PIECES))],
+        name="finish")(counts, gtok, *rest)
 
 def kernel_body(tokens, counts, bits, outgrad, g1, wqkv, wao, g2, win, wout, wdown, wup):
     bitsT, wdownT = bits.T, wdown.T
-    qkv, e, linv, ctx, hid, mlpin, act, slope, decoded, raw, mc = forward(counts, tokens, wqkv, wao, win, wout, g1, g2, wdownT, bitsT, wup)
-    gtok, loss, grads = backward(counts, raw, bitsT, wup, wdownT, g1, g2, mc, tokens, outgrad, wqkv, wao, win, wout, qkv, e, linv, ctx, hid, mlpin, act, slope)
+    gtok, loss, grads = train(counts, bitsT, wup, wdownT, g1, g2, tokens, outgrad, wqkv, wao, win, wout)[:3]
     scale = (tokens.shape[0] * lax.axis_size(("dp", "replica"))) ** -0.5
-    gtok, loss, gln1, gwqkv, gwao, gln2, gwin, gwout, gwdown, gwup = finish(scale, gtok, loss, wqkv, win, grads, wdownT, g1, g2)
+    decoded, gtok, loss, gln1, gwqkv, gwao, gln2, gwin, gwout, gwdown, gwup = finish(scale, counts, gtok, loss, wqkv, win, grads, wdownT, g1, g2, bitsT, wup)
     return (decoded, loss.reshape(()), gtok, gln1.reshape(24), gwqkv, gwao, gln2.reshape(24), gwin, gwout, gwdown, gwup)
 
 eps_norm = 1e-06

time: 169 us -> 149 us (0.88)
  Pallas kernels: 168 us -> 147 us
    pallas_call x2 -> x1, Pallas kernels: 161 us -> 140 us  [train(): pl.pallas_call(train_kernel, out_shape=[jax.ShapeDtypeStruct(*s) for s in...]
where the time goes in v3:
time: 149 us; the launch traced here: 148 us
  Pallas kernels  147 us (99%)
    pallas_call x1, Pallas kernels, train(): pl.pallas_call(train_kernel, out_shape=[jax.ShapeDtypeStruct(*s) for s in...  140 us
    pallas_call x1, Pallas kernels, finish(): pl.pallas_call(functools.partial(finish_kernel, scale), out_shape=[jax.Sh...  7.43 us

profile of v3, /device:TPU:0, one launch (start us, length us, event | category | flops | bytes accessed | tf_op | source)
XLA Modules:
  0.0 148.3 jit_solution(9524311184071483642)
XLA Ops:
  0.6 140.1 %train.1 = (f32[768,768]{1,0:T(8,128)}, f32[1,1]{1,0:T(1,128)}, f32[25,24,256]{2,1,0:T(8,128)}, bf16[2304,768]{1,0:T(8,128)(2,1)}, bf16[24,384,384]{2,1,0:T(8,128)(2,1)}, /*index=5*/f32[768,768]{1,0:T(8,128)}) custom-call(s32[64]{0:T(128)} %counts.3, s32[18,768]{1,0:T(8,128)} %bitcast.5, bf16[18,768]{1,0:T(8,128)(2,1)} %wup.3, bf16[18,768]{1,0:T(8,128)(2,1)} %bitcast.7, ...), custom_call_target="tpu_custom_call" | custom-call | tf_op jit(solution)/shard_map/train/pallas_call | solution.py:465
  140.7 7.4 %finish.1 = (f32[768,768]{1,0:T(8,128)}, f32[768,768]{1,0:T(8,128)}, f32[1,1]{1,0:T(1,128)}, f32[1,24]{1,0:T(1,128)}, f32[24,2304]{1,0:T(8,128)}, /*index=5*/f32...) custom-call(s32[64]{0:T(128)} %counts.3, ...), custom_call_target="tpu_custom_call" | custom-call | tf_op jit(solution)/shard_map/finish/pallas_call | solution.py:541

commit v4 on v3

--- a/solution.py
+++ b/solution.py
@@ -69,8 +69,8 @@
 
 def planar(k):
     if isinstance(k, int):
-        return int((k % 3 if k <= 12 else (k + 3) % 4) == 0)
-    return jnp.where(jnp.where(k <= 12, lax.rem(k, 3), lax.rem(k + 3, 4)) == 0, 1, 0)
+        return int(k >= 13 and (k + 3) % 4 != 0)
+    return jnp.where(k <= 12, 0, jnp.where(lax.rem(k + 3, 4) == 0, 0, 1))
 
 class Scatter:
     def __init__(self, bufs, result):
@@ -199,11 +199,11 @@
     lax.fori_loop(0, 6, fwd_ln1, 0)
     loads["wqkv"].wait()
     def proj(i, _):
-        v = dot(dattn[...], win[:, cols(i, 256)])
-        v = v * jnp.where(i < 3, 0.125, 1.0)
-        wout[pl.ds(pl.multiple_of(i // 3 * D, D), D), cols(i % 3, 256)] = v.astype(bf16)
-        return 0
-    lax.fori_loop(0, 9, proj, 0)
+        v = dot(dattn[...], win[:, cols(i, 768)])
+        v = v * jnp.where(i == 0, 0.125, 1.0)
+        wout[cols(i, D), :] = v.astype(bf16)
+        return 0
+    lax.fori_loop(0, 3, proj, 0)
     loads["win"].start()
     saves["qkv"].start()
     def heads_of(img, o):
@@ -253,14 +253,6 @@
     lax.fori_loop(0, 3, ao, 0)
     saves["linv"].wait()
     loads["outgrad"].start()
-    loads["wout"].wait()
-    def mcf(i, _):
-        r = cols(i, 768)
-        v = dot(wout[r, :], wd4t[...], 1, 1)
-        hi = v.astype(bf16).astype(f32)
-        mc[r, :] = jnp.where(lanes_of(768) % 64 < 32, hi, v - hi).astype(bf16)
-        return 0
-    lax.fori_loop(0, 4, mcf, 0)
     loads["win"].wait()
     for img in range(2):
         save_e(2, img).wait()
@@ -272,6 +264,14 @@
         slope[:, cs] = s.astype(bf16)
         return 0
     lax.fori_loop(0, FF // MC, fwd_mlp, 0)
+    loads["wout"].wait()
+    def mcf(i, _):
+        r = cols(i, 768)
+        v = dot(wout[r, :], wd4t[...], 1, 1)
+        hi = v.astype(bf16).astype(f32)
+        mc[r, :] = jnp.where(lanes_of(768) % 64 < 32, hi, v - hi).astype(bf16)
+        return 0
+    lax.fori_loop(0, 4, mcf, 0)
     rawv = dot(act[...], mc[...])
     raw[...] = rawv + pltpu.roll(rawv, 32, 1) + dot(hid[...].astype(bf16), wd4t[...], 1, 1)
     all_arrived()
@@ -346,7 +346,7 @@
             dp = (slope[:, cs].astype(f32) * d).astype(bf16)
             slope[:, cs] = dp
             main.late(t)
-            put(j, planar(j), dot(mlpinT[...], dp))
+            put(j, 0, dot(mlpinT[...], dp))
             main.early(t, j % 2)
         return 0
     lax.fori_loop(0, 2, mlp, 0)
@@ -361,7 +361,7 @@
         for j in range(1, 4):
             s = jnp.where(l4 == j, t[:, j], s)
         unit_s[b * 96:(b + 1) * 96, :] = s.reshape(96, 128)
-    main.put(0, 1, unit_s[...], 0)
+    main.put(0, 0, unit_s[...], 0)
     gwd = dot(drawT[...], hid[...].astype(bf16))
     for q in range(4):
         gv = big[128 * q:128 * q + 128, :]
@@ -373,7 +373,7 @@
     smallT[...] = jnp.where(r128 < 32, gwd, quantT[...])
     for i in range(6):
         unit_s[i * 128:(i + 1) * 128, :] = smallT[:, i * 128:(i + 1) * 128].T
-    main.put(0, 1, unit_s[...], 1)
+    main.put(0, 0, unit_s[...], 1)
     main.early(12, 0)
     loads["linv"].start()
     loads["qkv"].start()
@@ -405,7 +405,7 @@
     def group(g, _):
         t0 = 13 + 4 * g
         main.late(t0 + 1)
-        put(1, 1, dot(mlpinT[...], dattn[:, cols(g, W)]))
+        put(1, 0, dot(mlpinT[...], dattn[:, cols(g, W)]))
         main.early(t0, 1)
         def image(img, _):
             load_e(g, img).wait()
@@ -436,7 +436,7 @@
             return 0
         lax.fori_loop(0, 2, image, 0)
         for j in range(3):
-            put(j, 0, dot(ainT[...], act[:, pl.ds(pl.multiple_of(j * D + g * W, W), W)]))
+            put(j, 1, dot(ainT[...], act[:, pl.ds(pl.multiple_of(j * D + g * W, W), W)]))
             main.early(t0 + 1 + j, j % 2)
             if j == 1:
                 main.late(t0 + 4)
@@ -450,10 +450,11 @@
         dn = dot(act[r, :3 * D], win[:, :3 * D], 1, 1)
         nrm, inv = norm_stats(big[r, :])
         hid[r, :] += norm_back(dn, nrm, inv, g1[...].reshape(1, D))
+        main.late(27 + i)
         return 0
     lax.fori_loop(0, 3, ln1, 0)
     saves["gtok"].start()
-    for t in range(27, CHUNKS + LAGS[5]):
+    for t in range(30, CHUNKS + LAGS[5]):
         main.late(t)
     saves["gtok"].wait()
 
@@ -518,21 +519,17 @@
     gwdown[...] = other[:, :BITS]
     for r in reads: r.wait()
     odd = me % 2
-    def gain(weights, grad, lane_at, into):
+    own = lax.broadcasted_iota(jnp.int32, (24, D), 1) == lax.broadcasted_iota(jnp.int32, (24, D), 0) + me * 24
+    def gain(weights, grad, g, lane_at, into):
         w = weights[...].astype(f32)
         w = jnp.where(odd == 1, w[8:32], w[0:24])
-        return jnp.where(lane == lane_at, jnp.sum(w * grad[...], axis=1, keepdims=True), into)
-    flat = gain(wi, gwin, 65, gain(wq, gwqkv, 64, other))
+        mine = jnp.sum(jnp.where(own, g[...].reshape(1, D), 0.0), axis=1, keepdims=True)
+        return jnp.where(lane == lane_at, jnp.sum(w * grad[...], axis=1, keepdims=True) / mine, into)
+    flat = gain(wi, gwin, g2, 65, gain(wq, gwqkv, g1, 64, other))
     turned = jnp.concatenate([flat, jnp.zeros((104, 128), f32)], axis=0).T
     gwup[...] = turned[32:32 + BITS, :24]
-    def mine(g):
-        rows = jnp.broadcast_to(g[...].reshape(1, D), (8, D))
-        out = jnp.ones((8, 24), f32)
-        for i in range(32):
-            out = jnp.where(me == i, rows[:, 24 * i:24 * i + 24], out)
-        return out[0:1]
-    gln1[...] = (turned[64:65, :24] / mine(g1))
-    gln2[...] = (turned[65:66, :24] / mine(g2))
+    gln1[...] = turned[64:65, :24]
+    gln2[...] = turned[65:66, :24]
     for t in give + show: t.wait()
 
 def finish(scale, counts, gtok, *rest):

time: 149 us -> 141 us (0.946)
  Pallas kernels: 147 us -> 139 us
    pallas_call x1, Pallas kernels: 140 us -> 134 us  [train(): pl.pallas_call(train_kernel, out_shape=[jax.ShapeDtypeStruct(*s) for s in...]
where the time goes in v4:
time: 141 us; the launch traced here: 140 us
  Pallas kernels  139 us (99%)
    pallas_call x1, Pallas kernels, train(): pl.pallas_call(train_kernel, out_shape=[jax.ShapeDtypeStruct(*s) for s in...  134 us
    pallas_call x1, Pallas kernels, finish(): pl.pallas_call(functools.partial(finish_kernel, scale), out_shape=[jax.Sh...  5.96 us

profile of v4, /device:TPU:0, one launch (start us, length us, event | category | flops | bytes accessed | tf_op | source)
XLA Modules:
  0.0 140.3 jit_solution(11713052490370109837)
XLA Ops:
  0.6 133.5 %train.1 = (f32[768,768]{1,0:T(8,128)}, f32[1,1]{1,0:T(1,128)}, f32[25,24,256]{2,1,0:T(8,128)}, bf16[2304,768]{1,0:T(8,128)(2,1)}, bf16[24,384,384]{2,1,0:T(8,128)(2,1)}, /*index=5*/f32[768,768]{1,0:T(8,128)}) custom-call(s32[64]{0:T(128)} %counts.3, s32[18,768]{1,0:T(8,128)} %bitcast.5, bf16[18,768]{1,0:T(8,128)(2,1)} %wup.3, bf16[18,768]{1,0:T(8,128)(2,1)} %bitcast.7, ...), custom_call_target="tpu_custom_call" | custom-call | tf_op jit(solution)/shard_map/train/pallas_call | solution.py:466
  134.2 6.0 %finish.1 = (f32[768,768]{1,0:T(8,128)}, f32[768,768]{1,0:T(8,128)}, f32[1,1]{1,0:T(1,128)}, f32[1,24]{1,0:T(1,128)}, f32[24,2304]{1,0:T(8,128)}, /*index=5*/f32...) custom-call(s32[64]{0:T(128)} %counts.3, ...), custom_call_target="tpu_custom_call" | custom-call | tf_op jit(solution)/shard_map/finish/pallas_call | solution.py:538

commit v5 on v4

--- a/solution.py
+++ b/solution.py
@@ -42,7 +42,7 @@
 MESH = pl.DeviceIdType.MESH
 W = 256
 CHUNKS = 25
-LAGS = (0, 1, 6, 10, 13, 16)
+LAGS = (0, 1, 6, 10, 14, 18)
 
 def place():
     dp, rp = lax.axis_index("dp"), lax.axis_index("replica")
@@ -69,8 +69,8 @@
 
 def planar(k):
     if isinstance(k, int):
-        return int(k >= 13 and (k + 3) % 4 != 0)
-    return jnp.where(k <= 12, 0, jnp.where(lax.rem(k + 3, 4) == 0, 0, 1))
+        return int(k % 6 == 5 if k <= 12 else (k + 3) % 4 >= 2)
+    return jnp.where(k <= 12, jnp.where(lax.rem(k, 6) == 5, 1, 0), jnp.where(lax.rem(k + 3, 4) >= 2, 1, 0))
 
 class Scatter:
     def __init__(self, bufs, result):
@@ -80,7 +80,6 @@
     def route(self, k, h, n):
         z, x, y, c = self.at
         p, zl, zh = planar(k), z % 2, z // 2
-        tz = [(z + 1 - 2 * zl, 1 - p), (z + 2 - 4 * zh, 1 - p)]
         first, other = (x, y) if h == 0 else (y, x)
         def to(flip_first, flip_other, nz):
             f, o = first + flip_first * (1 - 2 * first), other + flip_other * (1 - 2 * other)
@@ -157,8 +156,8 @@
     mean = jnp.sum(gn, axis=1, keepdims=True) * (1.0 / D)
     return inv * (gn - mean - normed * spread)
 
-RB = 128
-MC = 512
+RB = 256
+MC = 1024
 def train_kernel(counts, bitsT, wup, wdownT, g1, g2, tokens_h, outgrad_h, wqkv_h, wao_h, win_h, wout_h,
                  gtok_h, loss_o, grads_o, qkv_h, e_h, linv_h,
                  hid, big, win, wout, wao, e, ctx, mlpin, act, slope, mlpinT, ainT, dattn, draw, drawT, unit_s, target, raw, mc,
@@ -192,11 +191,11 @@
     target[...] = wide[...].T
     loads["tokens"].wait()
     def fwd_ln1(i, _):
-        r = cols(i, 128)
+        r = cols(i, 256)
         n, _inv = norm_stats(hid[r, :])
         dattn[r, :] = (n * g1[...].reshape(1, D)).astype(bf16)
         return 0
-    lax.fori_loop(0, 6, fwd_ln1, 0)
+    lax.fori_loop(0, 3, fwd_ln1, 0)
     loads["wqkv"].wait()
     def proj(i, _):
         v = dot(dattn[...], win[:, cols(i, 768)])
@@ -346,7 +345,7 @@
             dp = (slope[:, cs].astype(f32) * d).astype(bf16)
             slope[:, cs] = dp
             main.late(t)
-            put(j, 0, dot(mlpinT[...], dp))
+            put(j, planar(j), dot(mlpinT[...], dp))
             main.early(t, j % 2)
         return 0
     lax.fori_loop(0, 2, mlp, 0)
@@ -361,7 +360,7 @@
         for j in range(1, 4):
             s = jnp.where(l4 == j, t[:, j], s)
         unit_s[b * 96:(b + 1) * 96, :] = s.reshape(96, 128)
-    main.put(0, 0, unit_s[...], 0)
+    main.put(0, planar(12), unit_s[...], 0)
     gwd = dot(drawT[...], hid[...].astype(bf16))
     for q in range(4):
         gv = big[128 * q:128 * q + 128, :]
@@ -373,7 +372,7 @@
     smallT[...] = jnp.where(r128 < 32, gwd, quantT[...])
     for i in range(6):
         unit_s[i * 128:(i + 1) * 128, :] = smallT[:, i * 128:(i + 1) * 128].T
-    main.put(0, 0, unit_s[...], 1)
+    main.put(0, planar(12), unit_s[...], 1)
     main.early(12, 0)
     loads["linv"].start()
     loads["qkv"].start()
@@ -405,7 +404,7 @@
     def group(g, _):
         t0 = 13 + 4 * g
         main.late(t0 + 1)
-        put(1, 0, dot(mlpinT[...], dattn[:, cols(g, W)]))
+        put(1, planar(13), dot(mlpinT[...], dattn[:, cols(g, W)]))
         main.early(t0, 1)
         def image(img, _):
             load_e(g, img).wait()
@@ -436,7 +435,7 @@
             return 0
         lax.fori_loop(0, 2, image, 0)
         for j in range(3):
-            put(j, 1, dot(ainT[...], act[:, pl.ds(pl.multiple_of(j * D + g * W, W), W)]))
+            put(j, planar(14 + j), dot(ainT[...], act[:, pl.ds(pl.multiple_of(j * D + g * W, W), W)]))
             main.early(t0 + 1 + j, j % 2)
             if j == 1:
                 main.late(t0 + 4)

time: 141 us -> 137 us (0.972)
  Pallas kernels: 139 us -> 136 us
    pallas_call x1, Pallas kernels: 134 us -> 130 us  [train(): pl.pallas_call(train_kernel, out_shape=[jax.ShapeDtypeStruct(*s) for s in...]
where the time goes in v5:
time: 137 us
  Pallas kernels  136 us (99%)
    pallas_call x1, Pallas kernels, train(): pl.pallas_call(train_kernel, out_shape=[jax.ShapeDtypeStruct(*s) for s in...  130 us
    pallas_call x1, Pallas kernels, finish(): pl.pallas_call(functools.partial(finish_kernel, scale), out_shape=[jax.Sh...  5.96 us

profile of v5, /device:TPU:0, one launch (start us, length us, event | category | flops | bytes accessed | tf_op | source)
XLA Modules:
  0.0 136.7 jit_solution(12690592816691611037)
XLA Ops:
  0.6 129.9 %train.1 = (f32[768,768]{1,0:T(8,128)}, f32[1,1]{1,0:T(1,128)}, f32[25,24,256]{2,1,0:T(8,128)}, bf16[2304,768]{1,0:T(8,128)(2,1)}, bf16[24,384,384]{2,1,0:T(8,128)(2,1)}, /*index=5*/f32[768,768]{1,0:T(8,128)}) custom-call(s32[64]{0:T(128)} %counts.3, s32[18,768]{1,0:T(8,128)} %bitcast.5, bf16[18,768]{1,0:T(8,128)(2,1)} %wup.3, bf16[18,768]{1,0:T(8,128)(2,1)} %bitcast.7, ...), custom_call_target="tpu_custom_call" | custom-call | tf_op jit(solution)/shard_map/train/pallas_call | solution.py:465
  130.6 6.0 %finish.1 = (f32[768,768]{1,0:T(8,128)}, f32[768,768]{1,0:T(8,128)}, f32[1,1]{1,0:T(1,128)}, f32[1,24]{1,0:T(1,128)}, f32[24,2304]{1,0:T(8,128)}, /*index=5*/f32...) custom-call(s32[64]{0:T(128)} %counts.3, ...), custom_call_target="tpu_custom_call" | custom-call | tf_op jit(solution)/shard_map/finish/pallas_call | solution.py:537

commit v6 on v5

--- a/solution.py
+++ b/solution.py
@@ -167,8 +167,12 @@
     main = Scatter(bufs, result)
     z, x, y, c = place()
     loads = {n: pltpu.make_async_copy(src, dst, sem.at[i]) for i, (n, src, dst) in enumerate((
-        ("tokens", tokens_h, hid), ("wqkv", wqkv_h, win.at[:, :3 * D]), ("wao", wao_h, wao), ("win", win_h, win), ("wout", wout_h, wout),
+        ("wao", wao_h, wao), ("win", win_h, win), ("wout", wout_h, wout),
         ("outgrad", outgrad_h, big), ("qkv", qkv_h, wout.at[:3 * D]), ("linv", linv_h, big), ("wqkv2", wqkv_h, win.at[:, :3 * D]), ("tokens2", tokens_h, big)))}
+    blocks = [pl.ds(i * 256, 256) for i in range(3)]
+    parts = [pl.ds(i * D, D) for i in range(3)]
+    rows_in = [pltpu.make_async_copy(tokens_h.at[b], hid.at[b], sem.at[8 + i]) for i, b in enumerate(blocks)]
+    cols_in = [pltpu.make_async_copy(wqkv_h.at[:, b], win.at[:, b], sem.at[11 + i]) for i, b in enumerate(parts)]
     saves = {n: pltpu.make_async_copy(src, dst, osem.at[i]) for i, (n, src, dst) in enumerate((
         ("qkv", wout.at[:3 * D], qkv_h), ("linv", big, linv_h), ("gtok", hid, gtok_h)))}
     def load_e(g, img):
@@ -176,8 +180,8 @@
     def save_e(g, img):
         return pltpu.make_async_copy(e.at[img], e_h.at[pl.ds(img * HEADS + g * 4, 4)], esem.at[2 + img])
     arrive()
-    for n in ("tokens", "wqkv", "wao"):
-        loads[n].start()
+    for l in rows_in + cols_in + [loads["wao"]]:
+        l.start()
     first = (lax.axis_index("dp") * lax.axis_size("replica") + lax.axis_index("replica")) * 2
     n0, n1 = counts[first], counts[first + 1]
     total = lax.fori_loop(0, counts.shape[0], lambda i, a: a + counts[i], jnp.int32(0)).astype(f32)
@@ -189,20 +193,14 @@
     wd4t[...] = wide[...].astype(bf16)
     widen(wide, (2.0 * bitsT[...].astype(f32) - 1.0) * BITS ** -0.5)
     target[...] = wide[...].T
-    loads["tokens"].wait()
-    def fwd_ln1(i, _):
-        r = cols(i, 256)
+    for l, r in zip(rows_in, blocks):
+        l.wait()
         n, _inv = norm_stats(hid[r, :])
         dattn[r, :] = (n * g1[...].reshape(1, D)).astype(bf16)
-        return 0
-    lax.fori_loop(0, 3, fwd_ln1, 0)
-    loads["wqkv"].wait()
-    def proj(i, _):
-        v = dot(dattn[...], win[:, cols(i, 768)])
-        v = v * jnp.where(i == 0, 0.125, 1.0)
-        wout[cols(i, D), :] = v.astype(bf16)
-        return 0
-    lax.fori_loop(0, 3, proj, 0)
+    for i, (l, b) in enumerate(zip(cols_in, parts)):
+        l.wait()
+        v = dot(dattn[...], win[:, b])
+        wout[b, :] = (v * 0.125 if i == 0 else v).astype(bf16)
     loads["win"].start()
     saves["qkv"].start()
     def heads_of(img, o):
@@ -470,7 +468,7 @@
             V((T, D), bf16), V((T, D), bf16), V((T, FF), bf16), V((T, FF), bf16), V((D, T), bf16), V((D, T), bf16), V((T, D), bf16),
             V((T, 128), bf16), V((128, T), bf16), V((T, 128), f32), V((T, 128), f32), V((T, 128), f32), V((FF, 128), bf16),
             V((128, D), f32), V((128, D), bf16), V((128, D), f32), V((128, D), f32), V((8, 8, 128), f32), V((4, 8, 128), f32),
-            S((10,)), S((3,)), S((10,)), S((10,)), S((4,))] + scatter_bufs(),
+            S((14,)), S((3,)), S((10,)), S((10,)), S((4,))] + scatter_bufs(),
         compiler_params=pltpu.CompilerParams(vmem_limit_bytes=64 << 20, collective_id=1, has_side_effects=True),
         name="train")(*args)
 

time: 137 us -> 137 us (level)
  no operation moved by 1% of the time
where the time goes in v6:
time: 137 us
  Pallas kernels  136 us (99%)
    pallas_call x1, Pallas kernels, train(): pl.pallas_call(train_kernel, out_shape=[jax.ShapeDtypeStruct(*s) for s in...  130 us
    pallas_call x1, Pallas kernels, finish(): pl.pallas_call(functools.partial(finish_kernel, scale), out_shape=[jax.Sh...  5.96 us

profile of v6, /device:TPU:0, one launch (start us, length us, event | category | flops | bytes accessed | tf_op | source)
XLA Modules:
  0.0 136.6 jit_solution(6036295717193685386)
XLA Ops:
  0.6 129.8 %train.1 = (f32[768,768]{1,0:T(8,128)}, f32[1,1]{1,0:T(1,128)}, f32[25,24,256]{2,1,0:T(8,128)}, bf16[2304,768]{1,0:T(8,128)(2,1)}, bf16[24,384,384]{2,1,0:T(8,128)(2,1)}, /*index=5*/f32[768,768]{1,0:T(8,128)}) custom-call(s32[64]{0:T(128)} %counts.3, s32[18,768]{1,0:T(8,128)} %bitcast.5, bf16[18,768]{1,0:T(8,128)(2,1)} %wup.3, bf16[18,768]{1,0:T(8,128)(2,1)} %bitcast.7, ...), custom_call_target="tpu_custom_call" | custom-call | tf_op jit(solution)/shard_map/train/pallas_call | solution.py:463
  130.4 6.0 %finish.1 = (f32[768,768]{1,0:T(8,128)}, f32[768,768]{1,0:T(8,128)}, f32[1,1]{1,0:T(1,128)}, f32[1,24]{1,0:T(1,128)}, f32[24,2304]{1,0:T(8,128)}, /*index=5*/f32...) custom-call(s32[64]{0:T(128)} %counts.3, ...), custom_call_target="tpu_custom_call" | custom-call | tf_op jit(solution)/shard_map/finish/pallas_call | solution.py:535
